TPU v7x, 512 devices: a whole 4x8x8 slice. The times are simulated.
512 devices in a mesh: vocab: 32 (over x, y), width: 16 (over z, core).
Axes of the slice: x: 4, y: 8, z: 8, core: 2. Of those that a mesh axis runs over, the one named last changes fastest.
Arguments:
- hidden: bfloat16 [448, 4608], P(None, 'width'), may hold values from -30 to 30
- head_weight: bfloat16 [65536, 4608], P('vocab', 'width'), may hold values from -0.09375 to 0.09375
- targets: int32 [448], replicated, may hold values from 0 to 65535
- lse_rest: float32 [448], replicated, may hold values from 18 to 23
- cotangent: float32 [448], replicated, may hold values from 0.3 to 3
Outputs:
- grad_hidden: bfloat16 [448, 4608], P(None, 'width')
- grad_weight: bfloat16 [65536, 4608], P('vocab', 'width')
- token_loss: float32 [448], P('width')
All inputs are finite; a program needn't handle non-finite values.
Results may differ from a plain program's by a relative error of at most 0.0051.
Values may be sent and summed in bfloat16 or wider, within the bound.
No kernel may reach another device: no remote copies, remote signals or barrier semaphores. Data moves between devices by JAX's collectives and lax.ppermute only.
A program may use at most 64 MiB of HBM per device.

v0:
```python
import jax
import jax.numpy as jnp
from jax import lax
from jax.sharding import PartitionSpec as P

soft_cap = 30.0
zloss_weight = 0.002


def row_logits(hidden, head_weight):
    return lax.dot_general(
        hidden, head_weight, (((1,), (1,)), ((), ())), preferred_element_type=jnp.float32
    )


def slab_grads(logits, row_targets, row_rest, row_cot):
    vocab_part = logits.shape[1]
    offset = lax.axis_index("vocab") * vocab_part
    capped = soft_cap * jnp.tanh(logits / soft_cap)
    local_ids = row_targets - offset
    columns = lax.broadcasted_iota(jnp.int32, (1, vocab_part), 1)
    onehot = (columns == local_ids[:, None]).astype(jnp.float32)
    exp_sum, picked = lax.psum(
        (jnp.sum(jnp.exp(capped), axis=1), jnp.sum(capped * onehot, axis=1)), "vocab"
    )
    lse = jnp.logaddexp(jnp.log(exp_sum), row_rest)
    token_loss = lse - picked + zloss_weight * lse * lse
    scale = 1.0 + 2.0 * zloss_weight * lse
    dcap = row_cot[:, None] * (jnp.exp(capped - lse[:, None]) * scale[:, None] - onehot)
    ratio = capped / soft_cap
    dlogit = (dcap * (1.0 - ratio * ratio)).astype(jnp.bfloat16)
    return (dlogit, token_loss)


def per_device(hidden, head_weight, targets, lse_rest, cotangent):
    tokens_all = hidden.shape[0]
    share = tokens_all // lax.axis_size("width")
    first = lax.axis_index("width") * share
    logits = lax.psum(row_logits(hidden, head_weight), "width")
    dlogit, losses = slab_grads(logits, targets, lse_rest, cotangent)
    token_loss = lax.dynamic_slice_in_dim(losses, first, share, 0)
    partial_grad = jnp.dot(dlogit, head_weight, preferred_element_type=jnp.float32)
    grad_hidden = lax.psum(partial_grad, "vocab").astype(jnp.bfloat16)
    grad_weight = lax.dot_general(
        dlogit, hidden, (((0,), (0,)), ((), ())), preferred_element_type=jnp.float32
    ).astype(jnp.bfloat16)
    return (grad_hidden, grad_weight, token_loss)


def solution(mesh):
    placed = (P(None, "width"), P("vocab", "width"), P(), P(), P())
    return jax.shard_map(
        per_device,
        mesh=mesh,
        in_specs=placed,
        out_specs=(P(None, "width"), P("vocab", "width"), P("width")),
        check_vma=False,
    )
```

profile of v0, /device:TPU:8, one launch (start us, length us, event | category | flops | bytes accessed | tf_op | source)
XLA Modules:
  0.0 376.9 jit_solution(114606909314989093)
XLA Ops:
  7.2 0.0 copy-start
  7.2 0.0 all-reduce.4.cloned.1.call-start
  7.2 1.2 copy-done
  8.4 3.9 %fusion.2 = f32[448,2048]{1,0:T(8,128)} fusion(bf16[448,288]{0,1:T(8,128)(2,1)} %param.5, bf16[2048,288]{0,1:T(8,128)(2,1)S(1)} %copy-done), kind=kOutput, calls=%fused_computation.12 | convolution fusion | flops 528482304 | bytes 5107712 | tf_op jit(solution)/shard_map/dot_general | solution.py:11
  12.4 0.0 copy-start.3
  12.4 0.0 copy-start.4
  12.4 0.0 copy-start.2
  12.4 0.0 all-reduce.4.cloned.1.call-update
  12.4 0.6 copy-done.3
  13.1 130.3 %all-reduce.4.cloned.1.call-done = f32[448,2048]{1,0:T(8,128)} async-done(((f32[448,2048]{1,0:T(8,128)}), f32[448,2048]{1,0:T(8,128)}) %all-reduce.4.cloned.1.call-update) | async-done | bytes 3670032 | tf_op jit(solution)/shard_map/psum | solution.py:39
  143.4 3.7 select_reduce_fusion
  147.1 71.2 %psum.29 = f32[448]{0:T(512)S(1)} all-reduce(f32[448]{0:T(512)S(1)} %get-tuple-element.4), channel_id=1, replica_groups=mesh['vocab'=32,'width'=16] {'vocab'}, use_global_device_ids=true, to_apply=%region_2.0 | all-reduce | flops 448 | bytes 3584 | tf_op jit(solution)/shard_map/psum | solution.py:23
  218.3 0.0 copy-done.4
  218.3 0.0 copy-done.2
  218.3 0.0 copy-start.1
  218.3 3.7 multiply_convert_fusion
  222.1 0.8 fusion.3
  222.9 0.0 copy-done.1
  222.9 1.8 convolution_convert_fusion
  224.7 144.7 %all-reduce.5 = (bf16[448,288]{0,1:T(8,128)(2,1)}, f32[448]{0:T(512)S(1)}) all-reduce(f32[448,288]{0,1:T(8,128)S(1)} %fusion.3, f32[448]{0:T(512)S(1)} %get-tuple-element.3), channel_id=1, replica_groups=mesh['vocab'=32,'width'=16] {'vocab'}, use_global_device_ids=true, to_apply=%region_3.0 | all-reduce | flops 129472 | bytes 777728 | tf_op jit(solution)/shard_map/psum | solution.py:43
  369.4 0.6 dynamic_slice.3
  (3 shorter events, 0.0 us)
Async XLA Ops:
  7.2 1.3 copy-start
  7.2 136.2 %all-reduce.4.cloned.1.call-start = ((), (), s32[]{:S(2)}) async-start(), calls=%async_computation | async-start | bytes 7340032 | tf_op jit(solution)/shard_map/psum | solution.py:39
  12.4 0.7 copy-start.3
  12.4 205.9 %copy-start.4 = (f32[448]{0:T(512)S(1)}, f32[448]{0:T(512)}, u32[]{:S(2)}) copy-start(f32[448]{0:T(512)} %param.8) | copy-start | bytes 5380
  12.4 205.9 %copy-start.2 = (f32[448]{0:T(512)S(1)}, f32[448]{0:T(512)}, u32[]{:S(2)}) copy-start(f32[448]{0:T(512)} %param.9) | copy-start | bytes 5380
  218.3 4.6 %copy-start.1 = (bf16[448,288]{0,1:T(8,128)(2,1)S(1)}, bf16[448,288]{0,1:T(8,128)(2,1)}, u32[]{:S(2)}) copy-start(bf16[448,288]{0,1:T(8,128)(2,1)} %param.5) | copy-start | bytes 774148
Sparse Core Ops, SparseCore 0:
  12.5 130.7 all-reduce.3
where the time goes:
time: 377 us
  blocking collectives  216 us (57%)
  waiting for transfers between devices  130 us (34%)
  between operations  14.1 us (4%)
  other arithmetic  7.47 us (2%)
  matrix products  6.57 us (2%)
    psum x1, blocking collectives, per_device(): grad_hidden = lax.psum(partial_grad, 'vocab').astype(jnp.bfloat16)  145 us
    psum x1, waiting for transfers between devices, per_device(): logits = lax.psum(row_logits(hidden, head_weight), 'width')  130 us
    psum x1, blocking collectives, slab_grads(): lax.psum((jnp.sum(jnp.exp(capped), axis=1), jnp.sum(capped * onehot, axis...  71.2 us
  transfers between devices with their start and end apart: 1, of which 1 were waited for; matrix products, arithmetic and copies ran while one was open for 0% of the time, Pallas kernels for 0%

commit v1 on v0

v1 whole, which is shorter than its diff:
```python
import jax
import jax.numpy as jnp
from jax import lax
from jax.experimental import pallas as pl
from jax.experimental.pallas import tpu as pltpu
from jax.sharding import Mesh, PartitionSpec as P

soft_cap = 30.0
zloss_weight = 0.002
wire = jnp.bfloat16
tokens = 448
lanes = 128


def params(**kw):
    return pltpu.CompilerParams(vmem_limit_bytes=32 * 1024 * 1024, **kw)


def half_logits(which, hidden_t, weight_t, received=None):
    depth = hidden_t.shape[0]

    def kernel(which_ref, h_ref, w_ref, *refs):
        out_ref, turned = refs[-2:]

        @pl.when(pl.program_id(0) == 0)
        def _():
            turned[...] = jnp.transpose(h_ref[...])

        part = jnp.dot(turned[...], w_ref[...], preferred_element_type=jnp.float32)
        for i in range(2):
            block = part[:, i * lanes : (i + 1) * lanes]
            if received is not None:
                block = block + refs[0][i].astype(jnp.float32)
            out_ref[i] = block.astype(wire)

    blocks = pl.BlockSpec((2, tokens, lanes), lambda i, c: (i, 0, 0))
    in_specs = [
        pl.BlockSpec((depth, tokens), lambda i, c: (0, 0)),
        pl.BlockSpec((depth, 2 * lanes), lambda i, c: (0, c[0] * 4 + i)),
    ]
    operands = [which, hidden_t, weight_t]
    if received is not None:
        in_specs.append(blocks)
        operands.append(received)
    return pl.pallas_call(
        kernel,
        grid_spec=pltpu.PrefetchScalarGridSpec(
            num_scalar_prefetch=1,
            grid=(4,),
            in_specs=in_specs,
            out_specs=blocks,
            scratch_shapes=[pltpu.VMEM((tokens, depth), jnp.bfloat16)],
        ),
        out_shape=jax.ShapeDtypeStruct((8, tokens, lanes), wire),
        compiler_params=params(),
    )(*operands)


def rows_of(vector):
    out = [vector[:, r * lanes : (r + 1) * lanes] for r in range(3)]
    tail = vector[:, 3 * lanes :]
    return out + [jnp.concatenate([tail, jnp.zeros((1, 4 * lanes - tokens), vector.dtype)], axis=1)]


def soften(first_column, parts, target_column):
    def kernel(first_ref, parts_ref, target_ref, out_ref):
        logits = parts_ref[0].astype(jnp.float32)
        for i in range(1, 8):
            logits = logits + parts_ref[i].astype(jnp.float32)
        ratio = jnp.tanh(logits * (1.0 / soft_cap))
        capped = soft_cap * ratio
        power = jnp.exp(capped - soft_cap)
        soft = (power * (1.0 - ratio * ratio)).astype(jnp.bfloat16)
        columns = lax.broadcasted_iota(jnp.int32, (tokens, lanes), 1) + first_ref[0]
        hit = jnp.where(columns == target_ref[...], capped, 0.0)
        ones = jnp.ones((8, lanes), jnp.float32)

        def total(block):
            return lax.dot_general(
                ones,
                block,
                (((1,), (1,)), ((), ())),
                precision=lax.Precision.HIGHEST,
                preferred_element_type=jnp.float32,
            )[0:1]

        row = lax.broadcasted_iota(jnp.int32, (16, lanes), 0)
        tile = jnp.zeros((16, lanes), jnp.float32)
        for k, sums in enumerate((total(power), total(hit))):
            for r, piece in enumerate(rows_of(sums)):
                high = piece.astype(jnp.bfloat16).astype(jnp.float32)
                tile = jnp.where(row == 8 * k + r, high, tile)
                tile = jnp.where(row == 8 * k + 4 + r, piece - high, tile)
        tile = tile.astype(jnp.bfloat16)
        for i in range(8):
            out_ref[i, :tokens] = soft
            out_ref[i, tokens:] = tile

    return pl.pallas_call(
        kernel,
        in_specs=[
            pl.BlockSpec(memory_space=pltpu.SMEM),
            pl.BlockSpec(memory_space=pltpu.VMEM),
            pl.BlockSpec(memory_space=pltpu.VMEM),
        ],
        out_specs=pl.BlockSpec(memory_space=pltpu.VMEM),
        out_shape=jax.ShapeDtypeStruct((8, tokens + 16, lanes), jnp.bfloat16),
        compiler_params=params(),
    )(first_column, parts, target_column)


def spread_sums(own, other):
    def kernel(own_ref, other_ref, out_ref):
        both = jnp.zeros((16, lanes), jnp.float32)
        for i in range(8):
            both = both + (own_ref[i].astype(jnp.float32) + other_ref[i].astype(jnp.float32))
        tile = jnp.concatenate([both[0:4] + both[4:8], both[8:12] + both[12:16]], axis=0)
        for i in range(32):
            out_ref[i] = tile

    spec = pl.BlockSpec((8, 16, lanes), lambda i: (0, tokens // 16, 0))
    return pl.pallas_call(
        kernel,
        grid=(1,),
        in_specs=[spec, spec],
        out_specs=pl.BlockSpec((32, 8, lanes), lambda i: (0, 0, 0)),
        out_shape=jax.ShapeDtypeStruct((32, 8, lanes), jnp.float32),
        compiler_params=params(),
    )(own, other)


def gradients(index, sums, rest_row, cot_row, target_column, own, other, hidden_t, weight_t):
    depth = hidden_t.shape[0]

    def kernel(
        index_ref, sums_ref, rest_ref, cot_ref, target_ref, own_ref, other_ref, h_ref, w_ref,
        gh_ref, gw_ref, loss_ref, total, factors,
    ):
        step = pl.program_id(0)

        @pl.when(step == 0)
        def _():
            tile = sums_ref[0]
            for i in range(1, 32):
                tile = tile + sums_ref[i]
            row = lax.broadcasted_iota(jnp.int32, (8, lanes), 0)
            rest = jnp.zeros((8, lanes), jnp.float32)
            cot = jnp.zeros((8, lanes), jnp.float32)
            for r, (a, b) in enumerate(zip(rows_of(rest_ref[...]), rows_of(cot_ref[...]))):
                rest = jnp.where(row == r, a, rest)
                cot = jnp.where((row == r) | (row == r + 4), b, cot)
            slab = jnp.log(tile) + soft_cap
            larger, smaller = jnp.maximum(slab, rest), jnp.minimum(slab, rest)
            lse = larger + jnp.log(1.0 + jnp.exp(smaller - larger))
            picked = jnp.concatenate([tile[4:8], tile[0:4]], axis=0)
            loss_ref[...] = lse - picked + zloss_weight * lse * lse
            scale = cot * (1.0 + 2.0 * zloss_weight * lse) * jnp.exp(soft_cap - lse)
            ratio = tile * (1.0 / soft_cap)
            hit = cot * (1.0 - ratio * ratio)
            turned = jnp.transpose(jnp.where(row < 4, scale, hit))
            for r in range(4):
                size = min(lanes, tokens - r * lanes)
                factors[r * lanes : r * lanes + size, 0:1] = turned[:size, r : r + 1]
                factors[r * lanes : r * lanes + size, 1:2] = turned[:size, r + 4 : r + 5]
            total[...] = jnp.zeros_like(total)

        half = jnp.where(step < 4, index_ref[0], 1 - index_ref[0])
        first = index_ref[1] + half * 8 * lanes + lax.rem(step, 4) * 2 * lanes
        scale, hit = factors[:, 0:1], factors[:, 1:2]
        blocks = []
        for i in range(2):
            block = jnp.where(step < 4, own_ref[i], other_ref[i]).astype(jnp.float32)
            columns = lax.broadcasted_iota(jnp.int32, (tokens, lanes), 1) + (first + i * lanes)
            onehot = jnp.where(columns == target_ref[...], hit, 0.0)
            blocks.append((block * scale - onehot).astype(jnp.bfloat16))
        dlogit = jnp.concatenate(blocks, axis=1)
        total[...] += lax.dot_general(
            dlogit, w_ref[...], (((1,), (1,)), ((), ())), preferred_element_type=jnp.float32
        )
        gw_ref[...] = jnp.dot(
            h_ref[...], dlogit, preferred_element_type=jnp.float32
        ).astype(jnp.bfloat16)

        @pl.when(step == 7)
        def _():
            gh_ref[:tokens] = total[...].astype(wire)
            gh_ref[tokens:] = jnp.zeros((512 - tokens, depth), wire)

    def whole(shape):
        return pl.BlockSpec(shape, lambda j, c: (0,) * len(shape))

    def vocab_block(j, c):
        half = jnp.where(j < 4, c[0], 1 - c[0])
        return (0, half * 4 + lax.rem(j, 4))

    return pl.pallas_call(
        kernel,
        grid_spec=pltpu.PrefetchScalarGridSpec(
            num_scalar_prefetch=1,
            grid=(8,),
            in_specs=[
                whole((32, 8, lanes)),
                whole((1, tokens)),
                whole((1, tokens)),
                whole((tokens, 1)),
                pl.BlockSpec((2, tokens, lanes), lambda j, c: (jnp.minimum(j, 3), 0, 0)),
                pl.BlockSpec((2, tokens, lanes), lambda j, c: (jnp.maximum(j - 4, 0), 0, 0)),
                whole((depth, tokens)),
                pl.BlockSpec((depth, 2 * lanes), vocab_block),
            ],
            out_specs=[
                whole((512, depth)),
                pl.BlockSpec((depth, 2 * lanes), vocab_block),
                whole((8, lanes)),
            ],
            scratch_shapes=[
                pltpu.VMEM((tokens, depth), jnp.float32),
                pltpu.VMEM((tokens, lanes), jnp.float32),
            ],
        ),
        out_shape=[
            jax.ShapeDtypeStruct((512, depth), wire),
            jax.ShapeDtypeStruct((depth, 2048), jnp.bfloat16),
            jax.ShapeDtypeStruct((8, lanes), jnp.float32),
        ],
        compiler_params=params(),
    )(index, sums, rest_row, cot_row, target_column, own, other, hidden_t, weight_t)


def add_and_spread(parts):
    def kernel(parts_ref, out_ref):
        total = parts_ref[0].astype(jnp.float32)
        for i in range(1, 32):
            total = total + parts_ref[i].astype(jnp.float32)
        total = total.astype(jnp.bfloat16)
        for i in range(32):
            out_ref[i] = total

    return pl.pallas_call(
        kernel,
        in_specs=[pl.BlockSpec(memory_space=pltpu.VMEM)],
        out_specs=pl.BlockSpec(memory_space=pltpu.VMEM),
        out_shape=jax.ShapeDtypeStruct(parts.shape, jnp.bfloat16),
        compiler_params=params(),
    )(parts)


def per_device(hidden, head_weight, targets, lse_rest, cotangent):
    x, y, z, core = (lax.axis_index(a) for a in ("x", "y", "z", "core"))
    swap = [(0, 1), (1, 0)]
    vocab_first = (x * 8 + y) * 2048
    first = vocab_first + core * 1024 + z * lanes
    index = jnp.stack([core, vocab_first]).astype(jnp.int32)
    target_column = targets.reshape(tokens, 1)
    hidden_t, weight_t = hidden.T, head_weight.T

    sent = half_logits((1 - core).reshape(1).astype(jnp.int32), hidden_t, weight_t)
    received = lax.ppermute(sent, "core", swap)
    mine = half_logits(core.reshape(1).astype(jnp.int32), hidden_t, weight_t, received)
    parts = lax.all_to_all(mine, "z", 0, 0, tiled=True)
    soft = soften(first.reshape(1).astype(jnp.int32), parts, target_column)
    own = lax.all_to_all(soft, "z", 0, 0, tiled=True)
    other = lax.ppermute(own, "core", swap)
    sums = lax.all_to_all(spread_sums(own, other), ("x", "y"), 0, 0, tiled=True)
    grad_part, grad_weight, losses = gradients(
        index,
        sums,
        lse_rest.reshape(1, tokens),
        cotangent.reshape(1, tokens),
        target_column,
        own,
        other,
        hidden_t,
        weight_t,
    )
    depth = hidden.shape[1]
    shares = lax.all_to_all(grad_part.reshape(32, 16, depth), ("x", "y"), 0, 0, tiled=True)
    whole = lax.all_to_all(add_and_spread(shares), ("x", "y"), 0, 0, tiled=True)
    grad_hidden = whole.reshape(512, depth)[:tokens]
    share = tokens // 16
    token_loss = lax.dynamic_slice_in_dim(losses.reshape(-1), (z * 2 + core) * share, share, 0)
    return (grad_hidden, grad_weight.T, token_loss)


def solution(mesh):
    mesh = Mesh(mesh.devices.reshape(4, 8, 8, 2), ("x", "y", "z", "core"))
    vocab, width = ("x", "y"), ("z", "core")
    return jax.shard_map(
        per_device,
        mesh=mesh,
        in_specs=(P(None, width), P(vocab, width), P(), P(), P()),
        out_specs=(P(None, width), P(vocab, width), P(width)),
        check_vma=False,
    )
```

time: 377 us -> 151 us (0.40)
  blocking collectives: 216 us -> 48.1 us
  waiting for transfers between devices: 130 us -> 53.9 us
  starting transfers between devices: 0.04 us -> 29.2 us
  between operations: 14.1 us -> 0.77 us
  Pallas kernels: 0 us -> 12.6 us
  other arithmetic: 7.47 us -> 0.08 us
  matrix products: 6.57 us -> 0 us
    psum x2 -> x0, blocking collectives: 216 us -> none  [the longest x1 145 us: per_device(): grad_hidden = lax.psum(partial_grad, 'vocab').astype(jnp.bfloat16)]
    psum x1 -> x0, waiting for transfers between devices: 130 us -> none  [per_device(): logits = lax.psum(row_logits(hidden, head_weight), 'width')]
    all_to_all x0 -> x3, waiting for transfers between devices: none -> 48.9 us  [the longest x1 26.1 us: per_device(): parts = lax.all_to_all(mine, 'z', 0, 0, tiled=True)]
    all_to_all x0 -> x2, blocking collectives: none -> 48.1 us  [the longest x1 29.5 us: per_device(): own = lax.all_to_all(soft, 'z', 0, 0, tiled=True)]
    all_to_all x0 -> x3, starting transfers between devices: none -> 25.3 us  [the longest x1 10.4 us: per_device(): parts = lax.all_to_all(mine, 'z', 0, 0, tiled=True)]
    pallas_call x0 -> x6, Pallas kernels: none -> 12.6 us  [the longest x1 7.06 us: gradients(): pl.pallas_call(kernel, grid_spec=pltpu.PrefetchScalarGridSpec(num_scalar_...]
    dot_general x3 -> x0, matrix products: 6.57 us -> none  [the longest x1 3.94 us: row_logits(): lax.dot_general(hidden, head_weight, (((1,), (1,)), ((), ())), preferred_...]
    ppermute x0 -> x2, waiting for transfers between devices: none -> 4.92 us  [the longest x1 2.49 us: per_device(): other = lax.ppermute(own, 'core', swap)]
  transfers between devices with their start and end apart: 1 -> 5, of which waited for: 1 -> 5; matrix products, arithmetic and copies ran while one was open for 0% -> 1% of each run, Pallas kernels for 0% -> 0%
where the time goes in v1:
time: 151 us
  waiting for transfers between devices  53.9 us (36%)
  blocking collectives  48.1 us (32%)
  starting transfers between devices  29.2 us (19%)
  Pallas kernels  12.6 us (8%)
  local copies, waits for them, and re-layouts  6.16 us (4%)
    all_to_all x1, blocking collectives, per_device(): own = lax.all_to_all(soft, 'z', 0, 0, tiled=True)  29.5 us
    all_to_all x1, waiting for transfers between devices, per_device(): parts = lax.all_to_all(mine, 'z', 0, 0, tiled=True)  26.1 us
    all_to_all x1, blocking collectives, per_device(): lax.all_to_all(grad_part.reshape(32, 16, depth), ('x', 'y'), 0, 0, tiled=...  18.6 us
    all_to_all x1, waiting for transfers between devices, per_device(): whole = lax.all_to_all(add_and_spread(shares), ('x', 'y'), 0, 0, tiled=True)  13 us
    all_to_all x1, starting transfers between devices, per_device(): parts = lax.all_to_all(mine, 'z', 0, 0, tiled=True)  10.4 us
    all_to_all x1, starting transfers between devices, per_device(): sums = lax.all_to_all(spread_sums(own, other), ('x', 'y'), 0, 0, tiled=True)  10.2 us
    all_to_all x1, waiting for transfers between devices, per_device(): sums = lax.all_to_all(spread_sums(own, other), ('x', 'y'), 0, 0, tiled=True)  9.92 us
    pallas_call x1, Pallas kernels, gradients(): pl.pallas_call(kernel, grid_spec=pltpu.PrefetchScalarGridSpec(num_scalar_...  7.06 us
  transfers between devices with their start and end apart: 5, of which 5 were waited for; matrix products, arithmetic and copies ran while one was open for 1% of the time, Pallas kernels for 0%

profile of v1, /device:TPU:8, one launch (start us, length us, event | category | flops | bytes accessed | tf_op | source)
XLA Modules:
  0.0 150.8 jit_solution(1128584281335338740)
XLA Ops:
  0.6 0.0 copy-start
  0.6 1.3 copy-done
  1.9 1.0 copy-done.2
  2.9 1.4 shard_map.76
  4.3 1.9 %collective-permute-start = (bf16[8,448,128]{2,1,0:T(8,128)(2,1)S(1)}, bf16[8,448,128]{2,1,0:T(8,128)(2,1)S(1)}, u32[]{:S(2)}, u32[]{:S(2)}) collective-permute-start(bf16[8,448,128]{2,1,0:T(8,128)(2,1)S(1)} %shard_map.76), channel_id=1, source_target_pairs={{0,1},{1,0},{2,3},{3,2},{4,5},{5,4},{6,7},{7,6},{8,9},{9,8},{10,11... | collective-permute-start | bytes 2752520 | tf_op jit(solution)/shard_map/ppermute | solution.py:258
  6.2 2.4 %collective-permute-done.refs_0_ = bf16[8,448,128]{2,1,0:T(8,128)(2,1)S(1)} collective-permute-done((bf16[8,448,128]{2,1,0:T(8,128)(2,1)S(1)}, bf16[8,448,128]{2,1,0:T(8,128)(2,1)S(1)}, u32[]{:S(2)}, u32[]{:S(2)}) %collective-permute-start) | collective-permute-done | bytes 917536 | tf_op jit(solution)/shard_map/ppermute | solution.py:258
  8.7 0.0 copy-done.1
  8.7 2.5 %shard_map.77 = bf16[8,448,128]{2,1,0:T(8,128)(2,1)} custom-call(s32[1]{0:T(128)} %bitcast.which_ref, bf16[288,448]{1,0:T(8,128)(2,1)S(1)} %bitcast.17, bf16[288,2048]{1,0:T(8,128)(2,1)S(1)} %bitcast.14, bf16[8,448,128]{2,1,0:T(8,128)(2,1)S(1)} %collective-permute-done.refs_0_), custom_call_target="tpu_custom_call" | custom-call | tf_op jit(solution)/shard_map/pallas_call | solution.py:45
  11.2 10.4 %all-to-all-start = ((bf16[8,448,128]{2,1,0:T(8,128)(2,1)}), bf16[8,448,128]{2,1,0:T(8,128)(2,1)S(1)}, u32[]{:S(2)}, u32[]{:S(2)}) async-start(bf16[8,448,128]{2,1,0:T(8,128)(2,1)} %shard_map.77), calls=%async_computation | async-start | bytes 1835008 | tf_op jit(solution)/shard_map/all_to_all | solution.py:260
  21.6 0.0 copy-done.9
  21.6 0.1 copy.9.target_ref
  21.8 26.1 %all-to-all-done.parts_ref = bf16[8,448,128]{2,1,0:T(8,128)(2,1)S(1)} async-done(((bf16[8,448,128]{2,1,0:T(8,128)(2,1)}), bf16[8,448,128]{2,1,0:T(8,128)(2,1)S(1)}, u32[]{:S(2)}, u32[]{:S(2)}) %all-to-all-start) | async-done | bytes 917536 | tf_op jit(solution)/shard_map/all_to_all | solution.py:260
  47.8 0.8 shard_map.78
  48.6 0.0 copy-start.4
  48.6 0.7 copy-done.4
  49.3 29.5 %all_to_all.25.own_ref = bf16[8,464,128]{2,1,0:T(8,128)(2,1)S(1)} all-to-all(bf16[8,464,128]{2,1,0:T(8,128)(2,1)S(1)} %shard_map.78), channel_id=1, replica_groups=mesh['x'=4,'y'=8,'z'=8,'core'=2] {'z'}, dimensions={0} | all-to-all | bytes 1900544 | tf_op jit(solution)/shard_map/all_to_all | solution.py:262
  78.8 2.0 %collective-permute-start.1 = (bf16[8,464,128]{2,1,0:T(8,128)(2,1)S(1)}, bf16[8,464,128]{2,1,0:T(8,128)(2,1)S(1)}, u32[]{:S(2)}, u32[]{:S(2)}) collective-permute-start(bf16[8,464,128]{2,1,0:T(8,128)(2,1)S(1)} %all_to_all.25.own_ref), channel_id=1, source_target_pairs={{0,1},{1,0},{2,3},{3,2},{4,5},{5,4},{6,7},{7,6},{8,9},{9,8},{10,11... | collective-permute-start | bytes 2850824 | tf_op jit(solution)/shard_map/ppermute | solution.py:263
  80.9 2.5 %collective-permute-done.1.other_ref = bf16[8,464,128]{2,1,0:T(8,128)(2,1)S(1)} collective-permute-done((bf16[8,464,128]{2,1,0:T(8,128)(2,1)S(1)}, bf16[8,464,128]{2,1,0:T(8,128)(2,1)S(1)}, u32[]{:S(2)}, u32[]{:S(2)}) %collective-permute-start.1) | collective-permute-done | bytes 950304 | tf_op jit(solution)/shard_map/ppermute | solution.py:263
  83.4 0.0 copy-start.6
  83.4 0.6 copy-done.6
  84.0 10.2 %all-to-all-start.2 = ((f32[32,8,128]{2,1,0:T(8,128)}), f32[32,8,128]{2,1,0:T(8,128)S(1)}, u32[]{:S(2)}, u32[]{:S(2)}) async-start(f32[32,8,128]{2,1,0:T(8,128)} %copy-done.6), calls=%async_computation.2 | async-start | bytes 262144 | tf_op jit(solution)/shard_map/all_to_all | solution.py:264
  94.2 0.1 pad_add_fusion.index_ref
  94.3 9.9 %all-to-all-done.2.sums_ref = f32[32,8,128]{2,1,0:T(8,128)S(1)} async-done(((f32[32,8,128]{2,1,0:T(8,128)}), f32[32,8,128]{2,1,0:T(8,128)S(1)}, u32[]{:S(2)}, u32[]{:S(2)}) %all-to-all-start.2) | async-done | bytes 131104 | tf_op jit(solution)/shard_map/all_to_all | solution.py:264
  104.2 0.0 copy-start.5
  104.2 0.9 copy-done.5
  105.2 7.1 %shard_map.80 = (bf16[512,288]{1,0:T(8,128)(2,1)S(1)}, bf16[288,2048]{1,0:T(8,128)(2,1)}, f32[8,128]{1,0:T(8,128)S(1)}) custom-call(s32[2]{0:T(128)S(1)} %pad_add_fusion.index_ref, f32[32,8,128]{2,1,0:T(8,128)S(1)} %all-to-all-done.2.sums_ref, f32[1,448]{1,0:T(1,128)S(1)} %bitcast.20, f32[1,448]{1,0:T(1,128)S(1)} %bitcast.21, s32[448,1]{1,0:T(8,128)S(1)} %copy-done.5, ...), custom_call_target="tpu_custom_call" | custom-call | tf_op jit(solution)/shard_map/pallas_call | solution.py:196
  112.2 18.6 %all_to_all.26.parts_ref = bf16[32,16,288]{2,1,0:T(8,128)(2,1)S(1)} all-to-all(bf16[32,16,288]{2,1,0:T(8,128)(2,1)S(1)} %bitcast.19), channel_id=1, replica_groups=mesh['x'=4,'y'=8,'z'=8,'core'=2] {'x','y'}, dimensions={0} | all-to-all | bytes 589824 | tf_op jit(solution)/shard_map/all_to_all | solution.py:277
  130.8 0.8 shard_map.81
  131.7 4.7 %all-to-all-start.4 = ((bf16[32,16,288]{2,1,0:T(8,128)(2,1)}), bf16[32,16,288]{2,1,0:T(8,128)(2,1)S(1)}, u32[]{:S(2)}, u32[]{:S(2)}) async-start(bf16[32,16,288]{2,1,0:T(8,128)(2,1)} %shard_map.81), calls=%async_computation.4 | async-start | bytes 786432 | tf_op jit(solution)/shard_map/all_to_all | solution.py:278
  136.3 0.6 dynamic_slice.3
  136.9 13.0 %all-to-all-done.4 = bf16[32,16,288]{2,1,0:T(8,128)(2,1)S(1)} async-done(((bf16[32,16,288]{2,1,0:T(8,128)(2,1)}), bf16[32,16,288]{2,1,0:T(8,128)(2,1)S(1)}, u32[]{:S(2)}, u32[]{:S(2)}) %all-to-all-start.4) | async-done | bytes 294944 | tf_op jit(solution)/shard_map/all_to_all | solution.py:278
  149.9 0.9 copy.11
  (11 shorter events, 0.1 us)
Async XLA Ops:
  0.6 1.3 copy-start
  1.9 1.0 copy-start.2
  2.9 5.8 %copy-start.1 = (bf16[2048,288]{0,1:T(8,128)(2,1)S(1)}, bf16[2048,288]{0,1:T(8,128)(2,1)}, u32[]{:S(2)}) copy-start(bf16[2048,288]{0,1:T(8,128)(2,1)} %param.6) | copy-start | bytes 3538948
  4.3 4.4 %collective-permute-start = (bf16[8,448,128]{2,1,0:T(8,128)(2,1)S(1)}, bf16[8,448,128]{2,1,0:T(8,128)(2,1)S(1)}, u32[]{:S(2)}, u32[]{:S(2)}) collective-permute-start(bf16[8,448,128]{2,1,0:T(8,128)(2,1)S(1)} %shard_map.76), channel_id=1, source_target_pairs={{0,1},{1,0},{2,3},{3,2},{4,5},{5,4},{6,7},{7,6},{8,9},{9,8},{10,11... | collective-permute-start | bytes 2752520 | tf_op jit(solution)/shard_map/ppermute | solution.py:258
  11.2 10.5 %copy-start.9 = (s32[448]{0:T(512)S(1)}, s32[448]{0:T(512)}, u32[]{:S(2)}) copy-start(s32[448]{0:T(512)} %param.7) | copy-start | bytes 5380
  11.2 36.7 %all-to-all-start = ((bf16[8,448,128]{2,1,0:T(8,128)(2,1)}), bf16[8,448,128]{2,1,0:T(8,128)(2,1)S(1)}, u32[]{:S(2)}, u32[]{:S(2)}) async-start(bf16[8,448,128]{2,1,0:T(8,128)(2,1)} %shard_map.77), calls=%async_computation | async-start | bytes 1835008 | tf_op jit(solution)/shard_map/all_to_all | solution.py:260
  48.6 0.7 copy-start.4
  78.8 25.4 %copy-start.3 = (bf16[448,288]{0,1:T(8,128)(2,1)S(1)}, bf16[448,288]{0,1:T(8,128)(2,1)}, u32[]{:S(2)}) copy-start(bf16[448,288]{0,1:T(8,128)(2,1)} %param.5) | copy-start | bytes 774148
  78.8 25.4 %copy-start.7 = (f32[448]{0:T(512)S(1)}, f32[448]{0:T(512)}, u32[]{:S(2)}) copy-start(f32[448]{0:T(512)} %param.8) | copy-start | bytes 5380
  78.8 25.4 %copy-start.8 = (f32[448]{0:T(512)S(1)}, f32[448]{0:T(512)}, u32[]{:S(2)}) copy-start(f32[448]{0:T(512)} %param.9) | copy-start | bytes 5380
  78.8 4.5 %collective-permute-start.1 = (bf16[8,464,128]{2,1,0:T(8,128)(2,1)S(1)}, bf16[8,464,128]{2,1,0:T(8,128)(2,1)S(1)}, u32[]{:S(2)}, u32[]{:S(2)}) collective-permute-start(bf16[8,464,128]{2,1,0:T(8,128)(2,1)S(1)} %all_to_all.25.own_ref), channel_id=1, source_target_pairs={{0,1},{1,0},{2,3},{3,2},{4,5},{5,4},{6,7},{7,6},{8,9},{9,8},{10,11... | collective-permute-start | bytes 2850824 | tf_op jit(solution)/shard_map/ppermute | solution.py:263
  83.4 0.7 copy-start.6
  84.0 20.2 %all-to-all-start.2 = ((f32[32,8,128]{2,1,0:T(8,128)}), f32[32,8,128]{2,1,0:T(8,128)S(1)}, u32[]{:S(2)}, u32[]{:S(2)}) async-start(f32[32,8,128]{2,1,0:T(8,128)} %copy-done.6), calls=%async_computation.2 | async-start | bytes 262144 | tf_op jit(solution)/shard_map/all_to_all | solution.py:264
  104.2 0.9 copy-start.5
  131.7 18.2 %all-to-all-start.4 = ((bf16[32,16,288]{2,1,0:T(8,128)(2,1)}), bf16[32,16,288]{2,1,0:T(8,128)(2,1)S(1)}, u32[]{:S(2)}, u32[]{:S(2)}) async-start(bf16[32,16,288]{2,1,0:T(8,128)(2,1)} %shard_map.81), calls=%async_computation.4 | async-start | bytes 786432 | tf_op jit(solution)/shard_map/all_to_all | solution.py:278

commit v2 on v0

v2 whole, which is shorter than its diff:
```python
import jax
import jax.numpy as jnp
from jax import lax
from jax.experimental import pallas as pl
from jax.experimental.pallas import tpu as pltpu
from jax.sharding import Mesh, PartitionSpec as P

soft_cap = 30.0
zloss_weight = 0.002
tokens = 448
lanes = 128
chunk = 16
shards = 32
filled = tokens // chunk
padded = 384
bf16, f32 = jnp.bfloat16, jnp.float32
vmem = pl.BlockSpec(memory_space=pltpu.VMEM)
smem = pl.BlockSpec(memory_space=pltpu.SMEM)


def call(kernel, out_shape, in_specs, scratch=()):
    several = isinstance(out_shape, (list, tuple))
    return pl.pallas_call(
        kernel,
        in_specs=in_specs,
        out_specs=[vmem] * len(out_shape) if several else vmem,
        out_shape=out_shape,
        scratch_shapes=scratch,
        compiler_params=pltpu.CompilerParams(vmem_limit_bytes=32 * 1024 * 1024),
    )


def iota(shape, axis):
    return lax.broadcasted_iota(jnp.int32, shape, axis)


def sent_logits(core, hidden_t, weight_t):
    def kernel(core_ref, h_ref, w_ref, out_ref):
        h = jnp.transpose(h_ref[...])
        for i in range(4):
            at = pl.multiple_of((1 - core_ref[0]) * 1024 + i * 256, 256)
            part = jnp.dot(h, w_ref[:, pl.ds(at, 256)], preferred_element_type=f32)
            out_ref[2 * i] = part[:, :lanes].astype(bf16)
            out_ref[2 * i + 1] = part[:, lanes:].astype(bf16)

    out = jax.ShapeDtypeStruct((8, tokens, lanes), bf16)
    return call(kernel, out, [smem, vmem, vmem])(core, hidden_t, weight_t)


def kept_logits(core, hidden_t, weight_t, received):
    def kernel(core_ref, h_ref, w_ref, got_ref, out_ref):
        h = jnp.transpose(h_ref[...])
        for i in range(4):
            at = pl.multiple_of(core_ref[0] * 1024 + i * 256, 256)
            part = jnp.dot(h, w_ref[:, pl.ds(at, 256)], preferred_element_type=f32)
            for k in range(2):
                block = part[:, k * lanes : (k + 1) * lanes] + got_ref[2 * i + k].astype(f32)
                out_ref[2 * i + k] = block.astype(bf16)

    out = jax.ShapeDtypeStruct((8, tokens, lanes), bf16)
    return call(kernel, out, [smem, vmem, vmem, vmem])(core, hidden_t, weight_t, received)


def high_low(tile):
    high = tile.astype(bf16).astype(f32)
    return [high, tile - high]


def soften(first_column, parts, target_column):
    def kernel(first_ref, parts_ref, target_ref, out_ref):
        logits = parts_ref[0].astype(f32)
        for i in range(1, 8):
            logits = logits + parts_ref[i].astype(f32)
        ratio = jnp.tanh(logits * (1.0 / soft_cap))
        capped = soft_cap * ratio
        power = jnp.exp(capped - soft_cap)
        soft = (power * (1.0 - ratio * ratio)).astype(bf16)
        hit = jnp.where(iota((tokens, lanes), 1) + first_ref[0] == target_ref[...], capped, 0.0)

        def total(block):
            return lax.dot_general(
                jnp.ones((8, lanes), f32),
                block,
                (((1,), (1,)), ((), ())),
                precision=lax.Precision.HIGHEST,
                preferred_element_type=f32,
            )[0:1]

        row = iota((16, lanes), 0)
        tile = jnp.zeros((16, lanes), f32)
        for k, sums in enumerate((total(power), total(hit))):
            pieces = [sums[:, r * lanes : (r + 1) * lanes] for r in range(3)]
            tail = jnp.zeros((1, 4 * lanes - tokens), f32)
            pieces.append(jnp.concatenate([sums[:, 3 * lanes :], tail], axis=1))
            for r, piece in enumerate(pieces):
                high, low = high_low(piece)
                tile = jnp.where(row == 8 * k + r, high, tile)
                tile = jnp.where(row == 8 * k + 4 + r, low, tile)
        tile = tile.astype(bf16)
        for i in range(8):
            out_ref[i, :tokens] = soft
            out_ref[i, tokens:] = tile

    out = jax.ShapeDtypeStruct((8, tokens + chunk, lanes), bf16)
    return call(kernel, out, [smem, vmem, vmem])(first_column, parts, target_column)


def columns_of(rows):
    turned = jnp.transpose(rows)
    out = []
    for at in range(0, rows.shape[0], 4):
        pieces = [turned[: min(lanes, tokens - r * lanes), at + r : at + r + 1] for r in range(4)]
        out.append(jnp.broadcast_to(jnp.concatenate(pieces, axis=0), (tokens, lanes)))
    return out


def unscaled(index, own, other, target_column, cot_rows, weight_t):
    depth = weight_t.shape[0]

    def kernel(index_ref, own_ref, other_ref, target_ref, cot_ref, w_ref, out_ref, hits, total):
        sums = jnp.zeros((chunk, lanes), f32)
        for i in range(8):
            sums = sums + (own_ref[i, tokens:].astype(f32) + other_ref[i, tokens:].astype(f32))
        powers, picked = sums[0:4] + sums[4:8], sums[8:12] + sums[12:16]
        ratio = picked * (1.0 / soft_cap)
        scale = cot_ref[...] * (1.0 - ratio * ratio)
        rows = high_low(powers) + high_low(picked) + [scale] * 4
        columns = columns_of(jnp.concatenate(rows, axis=0))
        hits[...] = columns[4]
        for j in range(8):
            which = index_ref[0] if j < 4 else 1 - index_ref[0]
            at = pl.multiple_of(which * 1024 + (j % 4) * 256, 256)
            blocks = []
            for k in range(2):
                place = 2 * (j % 4) + k
                soft = own_ref[place, :tokens] if j < 4 else other_ref[place, :tokens]
                column = iota((tokens, lanes), 1) + (index_ref[1] + at + k * lanes)
                hit = jnp.where(column == target_ref[...], hits[...], 0.0).astype(bf16)
                blocks.append(jnp.concatenate([soft, hit], axis=0))
            product = lax.dot_general(
                jnp.concatenate(blocks, axis=1),
                w_ref[:, pl.ds(at, 256)],
                (((1,), (1,)), ((), ())),
                preferred_element_type=f32,
            )
            if j == 0:
                total[...] = product
            else:
                total[...] += product
        lane = iota((tokens, lanes), 1)
        last = jnp.concatenate([total[:tokens, 256:], jnp.zeros((tokens, padded - depth), f32)], axis=1)
        for k in range(4):
            last = jnp.where(lane == depth - 256 + k, columns[k], last)
        out_ref[:filled, :chunk, :256] = total[:tokens, :256].astype(bf16).reshape(filled, chunk, 256)
        out_ref[:filled, :chunk, 256:] = last.astype(bf16).reshape(filled, chunk, lanes)
        out_ref[:filled, chunk:, :depth] = total[tokens:].astype(bf16).reshape(filled, chunk, depth)
        out_ref[:filled, chunk:, depth:] = jnp.zeros((filled, chunk, padded - depth), bf16)
        out_ref[filled:] = jnp.zeros((shards - filled, 2 * chunk, padded), bf16)

    return call(
        kernel,
        [
            jax.ShapeDtypeStruct((shards, 2 * chunk, padded), bf16),
            jax.ShapeDtypeStruct((tokens, lanes), f32),
        ],
        [smem, vmem, vmem, vmem, vmem, vmem],
        [pltpu.VMEM((2 * tokens, depth), f32)],
    )(index, own, other, target_column, cot_rows, weight_t)


def reduce_chunk(shard, parts, rest_and_cot, depth):
    def kernel(shard_ref, parts_ref, small_ref, out_ref):
        total = parts_ref[0].astype(f32)
        for i in range(1, shards):
            total = total + parts_ref[i].astype(f32)
        mine = small_ref[pl.ds(pl.multiple_of(shard_ref[0] * chunk, chunk), chunk)]
        rest, cot = mine[:, 0:1], mine[:, 1:2]
        power = total[:chunk, depth : depth + 1] + total[:chunk, depth + 1 : depth + 2]
        picked = total[:chunk, depth + 2 : depth + 3] + total[:chunk, depth + 3 : depth + 4]
        slab = jnp.log(power) + soft_cap
        larger, smaller = jnp.maximum(slab, rest), jnp.minimum(slab, rest)
        lse = larger + jnp.log(1.0 + jnp.exp(smaller - larger))
        loss = lse - picked + zloss_weight * lse * lse
        scale = cot * (1.0 + 2.0 * zloss_weight * lse) * jnp.exp(soft_cap - lse)
        out = total[:chunk] * scale - total[chunk:]
        lane = iota((chunk, padded), 1)
        for k, column in enumerate(high_low(scale) + high_low(loss)):
            out = jnp.where(lane == depth + k, column, out)
        out = out.astype(bf16)
        for i in range(shards):
            out_ref[i] = out

    out = jax.ShapeDtypeStruct((shards, chunk, padded), bf16)
    return call(kernel, out, [smem, vmem, vmem])(shard, parts, rest_and_cot)


def finish(index, reduced, own, other, hits, target_column, hidden_t):
    depth = hidden_t.shape[0]
    share = tokens // 16

    def kernel(
        index_ref, reduced_ref, own_ref, other_ref, hits_ref, target_ref, h_ref,
        gh_ref, gw_ref, loss_ref, scales, losses,
    ):
        last = reduced_ref[:filled, :, 256:].reshape(tokens, lanes).astype(f32)
        at = depth - 256
        scales[...] = jnp.broadcast_to(last[:, at : at + 1] + last[:, at + 1 : at + 2], (tokens, lanes))
        losses[:tokens] = jnp.broadcast_to(last[:, at + 2 : at + 3] + last[:, at + 3 : at + 4], (tokens, lanes))
        loss_ref[...] = jnp.transpose(losses[pl.ds(index_ref[2] * share, 32)])[0:1, :share]
        summed = reduced_ref[:filled].reshape(tokens, padded).astype(f32)
        gh_ref[...] = jnp.transpose(summed)[:depth].astype(bf16)
        for j in range(8):
            which = index_ref[0] if j < 4 else 1 - index_ref[0]
            at = pl.multiple_of(which * 1024 + (j % 4) * 256, 256)
            blocks = []
            for k in range(2):
                place = 2 * (j % 4) + k
                block = own_ref[place, :tokens] if j < 4 else other_ref[place, :tokens]
                column = iota((tokens, lanes), 1) + (index_ref[1] + at + k * lanes)
                hit = jnp.where(column == target_ref[...], hits_ref[...], 0.0)
                blocks.append((block.astype(f32) * scales[...] - hit).astype(bf16))
            product = jnp.dot(
                h_ref[...], jnp.concatenate(blocks, axis=1), preferred_element_type=f32
            )
            gw_ref[:, pl.ds(at, 256)] = product.astype(bf16)

    return call(
        kernel,
        [
            jax.ShapeDtypeStruct((depth, tokens), bf16),
            jax.ShapeDtypeStruct((depth, 2048), bf16),
            jax.ShapeDtypeStruct((1, share), f32),
        ],
        [smem] + [vmem] * 6,
        [pltpu.VMEM((tokens, lanes), f32), pltpu.VMEM((tokens + 32, lanes), f32)],
    )(index, reduced, own, other, hits, target_column, hidden_t)


def per_device(hidden, head_weight, targets, lse_rest, cotangent):
    x, y, z, core = (lax.axis_index(a).astype(jnp.int32) for a in ("x", "y", "z", "core"))
    swap = [(0, 1), (1, 0)]
    vocab = ("x", "y")
    shard = x * 8 + y
    index = jnp.stack([core, shard * 2048, z * 2 + core])
    first = (shard * 2048 + core * 1024 + z * lanes).reshape(1)
    target_column = targets.reshape(tokens, 1)
    rest_and_cot = jnp.pad(
        jnp.stack([lse_rest, cotangent], axis=1), ((0, shards * chunk - tokens), (0, 0))
    )
    cot_rows = jnp.pad(cotangent, (0, 4 * lanes - tokens)).reshape(4, lanes)
    hidden_t, weight_t = hidden.T, head_weight.T

    sent = sent_logits(index, hidden_t, weight_t)
    received = lax.ppermute(sent, "core", swap)
    mine = kept_logits(index, hidden_t, weight_t, received)
    parts = lax.all_to_all(mine, "z", 0, 0, tiled=True)
    own = lax.all_to_all(soften(first, parts, target_column), "z", 0, 0, tiled=True)
    other = lax.ppermute(own, "core", swap)
    part, hits = unscaled(index, own, other, target_column, cot_rows, weight_t)
    shares = lax.all_to_all(part, vocab, 0, 0, tiled=True)
    spread = reduce_chunk(shard.reshape(1), shares, rest_and_cot, hidden.shape[1])
    reduced = lax.all_to_all(spread, vocab, 0, 0, tiled=True)
    grad_hidden, grad_weight, token_loss = finish(
        index, reduced, own, other, hits, target_column, hidden_t
    )
    return (grad_hidden.T, grad_weight.T, token_loss.reshape(-1))


def solution(mesh):
    mesh = Mesh(mesh.devices.reshape(4, 8, 8, 2), ("x", "y", "z", "core"))
    vocab, width = ("x", "y"), ("z", "core")
    return jax.shard_map(
        per_device,
        mesh=mesh,
        in_specs=(P(None, width), P(vocab, width), P(), P(), P()),
        out_specs=(P(None, width), P(vocab, width), P(width)),
        check_vma=False,
    )
```

time: 377 us -> 144 us (0.38)
  blocking collectives: 216 us -> 49.1 us
  waiting for transfers between devices: 130 us -> 54 us
  starting transfers between devices: 0.04 us -> 24.6 us
  between operations: 14.1 us -> 0.8 us
  Pallas kernels: 0 us -> 10.5 us
  other arithmetic: 7.47 us -> 0.09 us
  matrix products: 6.57 us -> 0 us
    psum x2 -> x0, blocking collectives: 216 us -> none  [the longest x1 145 us: per_device(): grad_hidden = lax.psum(partial_grad, 'vocab').astype(jnp.bfloat16)]
    psum x1 -> x0, waiting for transfers between devices: 130 us -> none  [per_device(): logits = lax.psum(row_logits(hidden, head_weight), 'width')]
    all_to_all x0 -> x2, waiting for transfers between devices: none -> 49.1 us  [the longest x1 26.1 us: per_device(): parts = lax.all_to_all(mine, 'z', 0, 0, tiled=True)]
    all_to_all x0 -> x2, blocking collectives: none -> 49.1 us  [the longest x1 29.6 us: per_device(): lax.all_to_all(soften(first, parts, target_column), 'z', 0, 0, tiled=True)]
    all_to_all x0 -> x2, starting transfers between devices: none -> 20.7 us  [the longest x1 10.4 us: per_device(): parts = lax.all_to_all(mine, 'z', 0, 0, tiled=True)]
    pallas_call x0 -> x6, Pallas kernels: none -> 10.5 us  [the longest x1 3.12 us: finish(): call(kernel, [jax.ShapeDtypeStruct((depth, tokens), bf16), jax.ShapeDtype...]
    dot_general x3 -> x0, matrix products: 6.57 us -> none  [the longest x1 3.94 us: row_logits(): lax.dot_general(hidden, head_weight, (((1,), (1,)), ((), ())), preferred_...]
    ppermute x0 -> x2, waiting for transfers between devices: none -> 4.9 us  [the longest x1 2.46 us: per_device(): other = lax.ppermute(own, 'core', swap)]
  transfers between devices with their start and end apart: 1 -> 4, of which waited for: 1 -> 4; matrix products, arithmetic and copies ran while one was open for 0% -> 0% of each run, Pallas kernels for 0% -> 0%
where the time goes in v2:
time: 144 us; the launch traced here: 143 us
  waiting for transfers between devices  54 us (38%)
  blocking collectives  49.1 us (34%)
  starting transfers between devices  24.6 us (17%)
  Pallas kernels  10.5 us (7%)
  local copies, waits for them, and re-layouts  4.12 us (3%)
    all_to_all x1, blocking collectives, per_device(): lax.all_to_all(soften(first, parts, target_column), 'z', 0, 0, tiled=True)  29.6 us
    all_to_all x1, waiting for transfers between devices, per_device(): parts = lax.all_to_all(mine, 'z', 0, 0, tiled=True)  26.1 us
    all_to_all x1, waiting for transfers between devices, per_device(): shares = lax.all_to_all(part, vocab, 0, 0, tiled=True)  23.1 us
    all_to_all x1, blocking collectives, per_device(): reduced = lax.all_to_all(spread, vocab, 0, 0, tiled=True)  19.5 us
    all_to_all x1, starting transfers between devices, per_device(): parts = lax.all_to_all(mine, 'z', 0, 0, tiled=True)  10.4 us
    all_to_all x1, starting transfers between devices, per_device(): shares = lax.all_to_all(part, vocab, 0, 0, tiled=True)  10.3 us
    unnamed x20, local copies, waits for them, and re-layouts  3.82 us
    pallas_call x1, Pallas kernels, finish(): call(kernel, [jax.ShapeDtypeStruct((depth, tokens), bf16), jax.ShapeDtype...  3.12 us
  transfers between devices with their start and end apart: 4, of which 4 were waited for; matrix products, arithmetic and copies ran while one was open for 0% of the time, Pallas kernels for 0%

profile of v2, /device:TPU:8, one launch (start us, length us, event | category | flops | bytes accessed | tf_op | source)
XLA Modules:
  0.0 143.2 jit_solution(7166548880539779272)
XLA Ops:
  0.6 0.1 pad_add_fusion.core_ref.index_ref
  0.7 1.3 copy-done
  2.0 1.0 copy-done.2
  3.0 1.2 shard_map.76
  4.2 1.9 %collective-permute-start = (bf16[8,448,128]{2,1,0:T(8,128)(2,1)S(1)}, bf16[8,448,128]{2,1,0:T(8,128)(2,1)S(1)}, u32[]{:S(2)}, u32[]{:S(2)}) collective-permute-start(bf16[8,448,128]{2,1,0:T(8,128)(2,1)S(1)} %shard_map.76), channel_id=1, source_target_pairs={{0,1},{1,0},{2,3},{3,2},{4,5},{5,4},{6,7},{7,6},{8,9},{9,8},{10,11... | collective-permute-start | bytes 2752520 | tf_op jit(solution)/shard_map/ppermute | solution.py:254
  6.1 2.4 %collective-permute-done.got_ref = bf16[8,448,128]{2,1,0:T(8,128)(2,1)S(1)} collective-permute-done((bf16[8,448,128]{2,1,0:T(8,128)(2,1)S(1)}, bf16[8,448,128]{2,1,0:T(8,128)(2,1)S(1)}, u32[]{:S(2)}, u32[]{:S(2)}) %collective-permute-start) | collective-permute-done | bytes 917536 | tf_op jit(solution)/shard_map/ppermute | solution.py:254
  8.5 2.1 %shard_map.77 = bf16[8,448,128]{2,1,0:T(8,128)(2,1)} custom-call(s32[3]{0:T(128)S(1)} %pad_add_fusion.core_ref.index_ref, bf16[288,448]{1,0:T(8,128)(2,1)S(1)} %bitcast.19, bf16[288,2048]{1,0:T(8,128)(2,1)S(1)} %bitcast.16, bf16[8,448,128]{2,1,0:T(8,128)(2,1)S(1)} %collective-permute-done.got_ref), custom_call_target="tpu_custom_call" | custom-call | tf_op jit(solution)/shard_map/pallas_call | solution.py:61
  10.7 10.4 %all-to-all-start = ((bf16[8,448,128]{2,1,0:T(8,128)(2,1)}), bf16[8,448,128]{2,1,0:T(8,128)(2,1)S(1)}, u32[]{:S(2)}, u32[]{:S(2)}) async-start(bf16[8,448,128]{2,1,0:T(8,128)(2,1)} %shard_map.77), calls=%async_computation | async-start | bytes 1835008 | tf_op jit(solution)/shard_map/all_to_all | solution.py:256
  21.1 0.0 copy-done.8
  21.1 0.1 copy.13.target_ref
  21.3 26.1 %all-to-all-done.parts_ref = bf16[8,448,128]{2,1,0:T(8,128)(2,1)S(1)} async-done(((bf16[8,448,128]{2,1,0:T(8,128)(2,1)}), bf16[8,448,128]{2,1,0:T(8,128)(2,1)S(1)}, u32[]{:S(2)}, u32[]{:S(2)}) %all-to-all-start) | async-done | bytes 917536 | tf_op jit(solution)/shard_map/all_to_all | solution.py:256
  47.4 0.8 shard_map.78
  48.2 0.0 copy-start.7
  48.2 0.0 copy-start.1
  48.2 29.6 %all_to_all.20.own_ref = bf16[8,464,128]{2,1,0:T(8,128)(2,1)S(1)} all-to-all(bf16[8,464,128]{2,1,0:T(8,128)(2,1)S(1)} %shard_map.78), channel_id=1, replica_groups=mesh['x'=4,'y'=8,'z'=8,'core'=2] {'z'}, dimensions={0} | all-to-all | bytes 1900544 | tf_op jit(solution)/shard_map/all_to_all | solution.py:257
  77.8 1.9 %collective-permute-start.1 = (bf16[8,464,128]{2,1,0:T(8,128)(2,1)S(1)}, bf16[8,464,128]{2,1,0:T(8,128)(2,1)S(1)}, u32[]{:S(2)}, u32[]{:S(2)}) collective-permute-start(bf16[8,464,128]{2,1,0:T(8,128)(2,1)S(1)} %all_to_all.20.own_ref), channel_id=1, source_target_pairs={{0,1},{1,0},{2,3},{3,2},{4,5},{5,4},{6,7},{7,6},{8,9},{9,8},{10,11... | collective-permute-start | bytes 2850824 | tf_op jit(solution)/shard_map/ppermute | solution.py:258
  79.7 0.0 copy-done.7
  79.7 2.5 %collective-permute-done.1.other_ref = bf16[8,464,128]{2,1,0:T(8,128)(2,1)S(1)} collective-permute-done((bf16[8,464,128]{2,1,0:T(8,128)(2,1)S(1)}, bf16[8,464,128]{2,1,0:T(8,128)(2,1)S(1)}, u32[]{:S(2)}, u32[]{:S(2)}) %collective-permute-start.1) | collective-permute-done | bytes 950304 | tf_op jit(solution)/shard_map/ppermute | solution.py:258
  82.2 0.0 copy-done.1
  82.2 2.9 %shard_map.79 = (bf16[32,32,384]{2,1,0:T(8,128)(2,1)S(1)}, f32[448,128]{1,0:T(8,128)S(1)}) custom-call(s32[3]{0:T(128)S(1)} %pad_add_fusion.core_ref.index_ref, bf16[8,464,128]{2,1,0:T(8,128)(2,1)S(1)} %all_to_all.20.own_ref, bf16[8,464,128]{2,1,0:T(8,128)(2,1)S(1)} %collective-permute-done.1.other_ref, s32[448,1]{1,0:T(8,128)S(1)} %copy.13.target_ref, ...), custom_call_target="tpu_custom_call" | custom-call | tf_op jit(solution)/shard_map/pallas_call | solution.py:160
  85.1 0.0 copy-start.4
  85.2 0.9 copy-done.4
  86.0 0.7 copy-done.5
  86.7 10.3 %all-to-all-start.2 = ((bf16[32,32,384]{2,1,0:T(8,128)(2,1)}), bf16[32,32,384]{2,1,0:T(8,128)(2,1)S(1)}, u32[]{:S(2)}, u32[]{:S(2)}) async-start(bf16[32,32,384]{2,1,0:T(8,128)(2,1)} %copy-done.4), calls=%async_computation.2 | async-start | bytes 1572864 | tf_op jit(solution)/shard_map/all_to_all | solution.py:260
  97.0 0.0 copy-done.9
  97.0 0.1 copy.15
  97.2 0.0 copy-start.3
  97.2 23.1 %all-to-all-done.2.parts_ref = bf16[32,32,384]{2,1,0:T(8,128)(2,1)S(1)} async-done(((bf16[32,32,384]{2,1,0:T(8,128)(2,1)}), bf16[32,32,384]{2,1,0:T(8,128)(2,1)S(1)}, u32[]{:S(2)}, u32[]{:S(2)}) %all-to-all-start.2) | async-done | bytes 786464 | tf_op jit(solution)/shard_map/all_to_all | solution.py:260
  120.3 0.3 shard_map.80
  120.6 19.5 %all_to_all.21.reduced_ref = bf16[32,16,384]{2,1,0:T(8,128)(2,1)S(1)} all-to-all(bf16[32,16,384]{2,1,0:T(8,128)(2,1)S(1)} %shard_map.80), channel_id=1, replica_groups=mesh['x'=4,'y'=8,'z'=8,'core'=2] {'x','y'}, dimensions={0} | all-to-all | bytes 786432 | tf_op jit(solution)/shard_map/all_to_all | solution.py:262
  140.1 0.0 copy-done.3
  140.1 3.1 %shard_map.81 = (bf16[288,448]{1,0:T(8,128)(2,1)}, bf16[288,2048]{1,0:T(8,128)(2,1)}, f32[1,28]{1,0:T(1,128)}) custom-call(s32[3]{0:T(128)S(1)} %pad_add_fusion.core_ref.index_ref, bf16[32,16,384]{2,1,0:T(8,128)(2,1)S(1)} %all_to_all.21.reduced_ref, bf16[8,464,128]{2,1,0:T(8,128)(2,1)S(1)} %all_to_all.20.own_ref, ...), custom_call_target="tpu_custom_call" | custom-call | tf_op jit(solution)/shard_map/pallas_call | solution.py:227
  (10 shorter events, 0.0 us)
Async XLA Ops:
  0.7 1.3 copy-start
  2.0 1.0 copy-start.2
  4.2 4.4 %collective-permute-start = (bf16[8,448,128]{2,1,0:T(8,128)(2,1)S(1)}, bf16[8,448,128]{2,1,0:T(8,128)(2,1)S(1)}, u32[]{:S(2)}, u32[]{:S(2)}) collective-permute-start(bf16[8,448,128]{2,1,0:T(8,128)(2,1)S(1)} %shard_map.76), channel_id=1, source_target_pairs={{0,1},{1,0},{2,3},{3,2},{4,5},{5,4},{6,7},{7,6},{8,9},{9,8},{10,11... | collective-permute-start | bytes 2752520 | tf_op jit(solution)/shard_map/ppermute | solution.py:254
  10.7 10.5 %copy-start.8 = (s32[448]{0:T(512)S(1)}, s32[448]{0:T(512)}, u32[]{:S(2)}) copy-start(s32[448]{0:T(512)} %param.7) | copy-start | bytes 5380
  10.7 36.7 %all-to-all-start = ((bf16[8,448,128]{2,1,0:T(8,128)(2,1)}), bf16[8,448,128]{2,1,0:T(8,128)(2,1)S(1)}, u32[]{:S(2)}, u32[]{:S(2)}) async-start(bf16[8,448,128]{2,1,0:T(8,128)(2,1)} %shard_map.77), calls=%async_computation | async-start | bytes 1835008 | tf_op jit(solution)/shard_map/all_to_all | solution.py:256
  48.2 31.6 %copy-start.7 = (f32[448]{0:T(512)S(1)}, f32[448]{0:T(512)}, u32[]{:S(2)}) copy-start(f32[448]{0:T(512)} %param.9) | copy-start | bytes 5380
  48.2 34.0 %copy-start.1 = (bf16[2048,288]{0,1:T(8,128)(2,1)S(1)}, bf16[2048,288]{0,1:T(8,128)(2,1)}, u32[]{:S(2)}) copy-start(bf16[2048,288]{0,1:T(8,128)(2,1)} %param.6) | copy-start | bytes 3538948
  77.8 4.4 %collective-permute-start.1 = (bf16[8,464,128]{2,1,0:T(8,128)(2,1)S(1)}, bf16[8,464,128]{2,1,0:T(8,128)(2,1)S(1)}, u32[]{:S(2)}, u32[]{:S(2)}) collective-permute-start(bf16[8,464,128]{2,1,0:T(8,128)(2,1)S(1)} %all_to_all.20.own_ref), channel_id=1, source_target_pairs={{0,1},{1,0},{2,3},{3,2},{4,5},{5,4},{6,7},{7,6},{8,9},{9,8},{10,11... | collective-permute-start | bytes 2850824 | tf_op jit(solution)/shard_map/ppermute | solution.py:258
  85.1 0.9 copy-start.4
  86.0 0.7 copy-start.5
  86.7 10.3 %copy-start.9 = (f32[448]{0:T(512)S(1)}, f32[448]{0:T(512)}, u32[]{:S(2)}) copy-start(f32[448]{0:T(512)} %param.8) | copy-start | bytes 5380
  86.7 33.6 %all-to-all-start.2 = ((bf16[32,32,384]{2,1,0:T(8,128)(2,1)}), bf16[32,32,384]{2,1,0:T(8,128)(2,1)S(1)}, u32[]{:S(2)}, u32[]{:S(2)}) async-start(bf16[32,32,384]{2,1,0:T(8,128)(2,1)} %copy-done.4), calls=%async_computation.2 | async-start | bytes 1572864 | tf_op jit(solution)/shard_map/all_to_all | solution.py:260
  97.2 42.9 %copy-start.3 = (bf16[448,288]{0,1:T(8,128)(2,1)S(1)}, bf16[448,288]{0,1:T(8,128)(2,1)}, u32[]{:S(2)}) copy-start(bf16[448,288]{0,1:T(8,128)(2,1)} %param.5) | copy-start | bytes 774148
  120.3 19.8 %copy-start.6 = (f32[448,128]{1,0:T(8,128)S(1)}, f32[448,128]{1,0:T(8,128)}, u32[]{:S(2)}) copy-start(f32[448,128]{1,0:T(8,128)} %copy-done.5) | copy-start | bytes 688132

commit v3 on v2

v3 whole, which is shorter than its diff:
```python
import jax
import jax.numpy as jnp
from jax import lax
from jax.experimental import pallas as pl
from jax.experimental.pallas import tpu as pltpu
from jax.sharding import Mesh, PartitionSpec as P

soft_cap = 30.0
zloss_weight = 0.002
tokens = 448
lanes = 128
chunk = 16
shards = 32
filled = tokens // chunk
padded = 384
packed = 640
bf16, f32 = jnp.bfloat16, jnp.float32
vmem = pl.BlockSpec(memory_space=pltpu.VMEM)
smem = pl.BlockSpec(memory_space=pltpu.SMEM)


def call(kernel, out_shape, in_specs, scratch=()):
    several = isinstance(out_shape, (list, tuple))
    return pl.pallas_call(
        kernel,
        in_specs=in_specs,
        out_specs=[vmem] * len(out_shape) if several else vmem,
        out_shape=out_shape,
        scratch_shapes=scratch,
        compiler_params=pltpu.CompilerParams(vmem_limit_bytes=32 * 1024 * 1024),
    )


def iota(shape, axis):
    return lax.broadcasted_iota(jnp.int32, shape, axis)


def rows_of(vector):
    out = [vector[:, r * lanes : (r + 1) * lanes] for r in range(3)]
    tail = jnp.zeros((1, 4 * lanes - tokens), vector.dtype)
    return out + [jnp.concatenate([vector[:, 3 * lanes :], tail], axis=1)]


def columns_of(rows):
    turned = jnp.transpose(rows)
    out = []
    for at in range(0, rows.shape[0], 4):
        pieces = [turned[: min(lanes, tokens - r * lanes), at + r : at + r + 1] for r in range(4)]
        out.append(jnp.broadcast_to(jnp.concatenate(pieces, axis=0), (tokens, lanes)))
    return out


def half_logits(index, hidden_t, weight_t, vectors=()):
    depth = hidden_t.shape[0]
    own = bool(vectors)
    kind = f32 if own else bf16

    def kernel(index_ref, h_ref, w_ref, *refs):
        turned = refs[-1]
        out_ref = refs[3] if own else refs[0]

        @pl.when(pl.program_id(0) == 0)
        def _():
            turned[...] = jnp.transpose(h_ref[...])
            if own:
                target_ref, rest_ref, cot_ref = refs[:3]
                rows = rows_of(target_ref[...].astype(f32)) + rows_of(rest_ref[...]) + rows_of(cot_ref[...])
                tile = jnp.zeros((16, lanes), f32)
                for r, row in enumerate(rows):
                    tile = jnp.where(iota((16, lanes), 0) == r, row, tile)
                target, rest, cot, _ = columns_of(tile)
                refs[4][...] = target
                refs[5][:tokens] = jnp.where(iota((tokens, lanes), 1) == 0, rest, cot)
                refs[5][tokens:] = jnp.zeros((shards * chunk - tokens, lanes), f32)

        part = jnp.dot(turned[...], w_ref[...], preferred_element_type=f32).astype(kind)
        out_ref[0] = part[:, :lanes]
        out_ref[1] = part[:, lanes:]

    def whole(*shape):
        return pl.BlockSpec(shape, lambda i, c: (0,) * len(shape))

    def block(i, c):
        return (0, (c[0] if own else 1 - c[0]) * 4 + i)

    out_specs = [pl.BlockSpec((2, tokens, lanes), lambda i, c: (i, 0, 0))]
    out_shape = [jax.ShapeDtypeStruct((8, tokens, lanes), kind)]
    if own:
        out_specs += [whole(tokens, lanes), whole(shards * chunk, lanes)]
        out_shape += [jax.ShapeDtypeStruct(spec.block_shape, f32) for spec in out_specs[1:]]
    return pl.pallas_call(
        kernel,
        grid_spec=pltpu.PrefetchScalarGridSpec(
            num_scalar_prefetch=1,
            grid=(4,),
            in_specs=[whole(depth, tokens), pl.BlockSpec((depth, 256), block)]
            + [whole(1, tokens)] * len(vectors),
            out_specs=out_specs,
            scratch_shapes=[pltpu.VMEM((tokens, depth), bf16)],
        ),
        out_shape=out_shape,
        compiler_params=pltpu.CompilerParams(vmem_limit_bytes=(32 if own else 60) * 1024 * 1024),
    )(index, hidden_t, weight_t, *vectors)


def add_halves(kept, received):
    def kernel(kept_ref, received_ref, out_ref):
        for i in range(8):
            out_ref[i] = (kept_ref[i] + received_ref[i].astype(f32)).astype(bf16)

    return call(kernel, jax.ShapeDtypeStruct(kept.shape, bf16), [vmem, vmem])(kept, received)


def high_low(tile):
    high = tile.astype(bf16).astype(f32)
    return [high, tile - high]


def soften(index, parts, target):
    def kernel(index_ref, parts_ref, target_ref, out_ref):
        logits = parts_ref[0].astype(f32)
        for i in range(1, 8):
            logits = logits + parts_ref[i].astype(f32)
        ratio = jnp.tanh(logits * (1.0 / soft_cap))
        capped = soft_cap * ratio
        power = jnp.exp(capped - soft_cap)
        soft = (power * (1.0 - ratio * ratio)).astype(bf16)
        first = index_ref[1] + index_ref[0] * 1024 + (index_ref[2] // 2) * lanes
        columns = (iota((tokens, lanes), 1) + first).astype(f32)
        hit = jnp.where(columns == target_ref[...], capped, 0.0)

        def total(block):
            return lax.dot_general(
                jnp.ones((8, lanes), f32),
                block,
                (((1,), (1,)), ((), ())),
                precision=lax.Precision.HIGHEST,
                preferred_element_type=f32,
            )[0:1]

        row = iota((16, lanes), 0)
        tile = jnp.zeros((16, lanes), f32)
        for k, sums in enumerate((total(power), total(hit))):
            for r, piece in enumerate(rows_of(sums)):
                high, low = high_low(piece)
                tile = jnp.where(row == 8 * k + r, high, tile)
                tile = jnp.where(row == 8 * k + 4 + r, low, tile)
        tile = tile.astype(bf16)
        for i in range(8):
            out_ref[i, :tokens] = soft
            out_ref[i, tokens:] = tile

    out = jax.ShapeDtypeStruct((8, tokens + chunk, lanes), bf16)
    return call(kernel, out, [smem, vmem, vmem])(index, parts, target)


def half_grad(index, soft, target, small, weight_t, before=()):
    depth = weight_t.shape[0]
    last = bool(before)

    def kernel(index_ref, soft_ref, target_ref, small_ref, w_ref, *refs):
        sums = jnp.zeros((chunk, lanes), f32)
        for i in range(8):
            sums = sums + soft_ref[i, tokens:].astype(f32)
        if last:
            sums = sums + refs[1][...]
        rows = [sums[0:4] + sums[4:8], sums[8:12] + sums[12:16]]
        power, picked = columns_of(jnp.concatenate(rows, axis=0))
        ratio = picked * (1.0 / soft_cap)
        cot = jnp.broadcast_to(small_ref[:tokens, 1:2], (tokens, lanes))
        hits = cot * (1.0 - ratio * ratio)
        total = refs[-1]
        which = 1 - index_ref[0] if last else index_ref[0]
        for j in range(4):
            at = pl.multiple_of(which * 1024 + j * 256, 256)
            blocks = []
            for k in range(2):
                column = (iota((tokens, lanes), 1) + (index_ref[1] + at + k * lanes)).astype(f32)
                hit = jnp.where(column == target_ref[...], hits, 0.0).astype(bf16)
                blocks.append(jnp.concatenate([soft_ref[2 * j + k, :tokens], hit], axis=0))
            product = lax.dot_general(
                jnp.concatenate(blocks, axis=1),
                w_ref[:, pl.ds(at, 256)],
                (((1,), (1,)), ((), ())),
                preferred_element_type=f32,
            )
            if j:
                total[...] += product
            elif last:
                total[...] = refs[0][...] + product
            else:
                total[...] = product
        if not last:
            refs[1][...] = sums
            return
        out_ref, hits_ref = refs[2:4]
        hits_ref[...] = hits
        first, second = total[:tokens], total[tokens:]
        lane = iota((tokens, lanes), 1)
        end = jnp.concatenate([second[:, 224:], jnp.zeros((tokens, lanes - depth + 224), f32)], axis=1)
        for k, column in enumerate(high_low(power) + high_low(picked)):
            end = jnp.where(lane == depth - 224 + k, column, end)
        middle = jnp.concatenate([first[:, 256:], second[:, :96]], axis=1)
        for t, piece in enumerate((first[:, :lanes], first[:, lanes:256], middle, second[:, 96:224], end)):
            out_ref[:filled, :, t * lanes : (t + 1) * lanes] = piece.astype(bf16).reshape(filled, chunk, lanes)
        out_ref[filled:] = jnp.zeros((shards - filled, chunk, packed), bf16)

    total = (2 * tokens, depth)
    if last:
        out = [
            jax.ShapeDtypeStruct((shards, chunk, packed), bf16),
            jax.ShapeDtypeStruct((tokens, lanes), f32),
        ]
        scratch = [pltpu.VMEM(total, f32)]
    else:
        out = [jax.ShapeDtypeStruct((chunk, lanes), f32), jax.ShapeDtypeStruct(total, f32)]
        out = [out[1], out[0]]
        scratch = []
    inside = kernel if last else lambda *refs: kernel(*refs, refs[5])
    return call(inside, out, [smem] + [vmem] * (4 + len(before)), scratch)(
        index, soft, target, small, weight_t, *before
    )


def reduce_chunk(index, parts, small, depth):
    def kernel(index_ref, parts_ref, small_ref, out_ref):
        total = parts_ref[0].astype(f32)
        for i in range(1, shards):
            total = total + parts_ref[i].astype(f32)
        mine = small_ref[pl.ds(pl.multiple_of(index_ref[3] * chunk, chunk), chunk)]
        rest, cot = mine[:, 0:1], mine[:, 1:2]
        at = 2 * depth
        power = total[:, at : at + 1] + total[:, at + 1 : at + 2]
        picked = total[:, at + 2 : at + 3] + total[:, at + 3 : at + 4]
        slab = jnp.log(power) + soft_cap
        larger, smaller = jnp.maximum(slab, rest), jnp.minimum(slab, rest)
        lse = larger + jnp.log(1.0 + jnp.exp(smaller - larger))
        loss = lse - picked + zloss_weight * lse * lse
        scale = cot * (1.0 + 2.0 * zloss_weight * lse) * jnp.exp(soft_cap - lse)
        out = total[:, :depth] * scale - total[:, depth:at]
        out = jnp.concatenate([out, jnp.zeros((chunk, padded - depth), f32)], axis=1)
        lane = iota((chunk, padded), 1)
        for k, column in enumerate(high_low(scale) + high_low(loss)):
            out = jnp.where(lane == depth + k, column, out)
        out = out.astype(bf16)
        for i in range(shards):
            out_ref[i] = out

    out = jax.ShapeDtypeStruct((shards, chunk, padded), bf16)
    return call(kernel, out, [smem, vmem, vmem])(index, parts, small)


def finish(index, reduced, own, other, hits, target, hidden_t):
    depth = hidden_t.shape[0]
    share = tokens // 16

    def kernel(
        index_ref, reduced_ref, own_ref, other_ref, hits_ref, target_ref, h_ref,
        gh_ref, gw_ref, loss_ref, scales, losses,
    ):
        last = reduced_ref[:filled, :, 256:].reshape(tokens, lanes).astype(f32)
        at = depth - 256
        scales[...] = jnp.broadcast_to(last[:, at : at + 1] + last[:, at + 1 : at + 2], (tokens, lanes))
        losses[:tokens] = jnp.broadcast_to(last[:, at + 2 : at + 3] + last[:, at + 3 : at + 4], (tokens, lanes))
        loss_ref[...] = jnp.transpose(losses[pl.ds(index_ref[2] * share, 32)])[0:1, :share]
        summed = reduced_ref[:filled].reshape(tokens, padded).astype(f32)
        gh_ref[...] = jnp.transpose(summed)[:depth].astype(bf16)
        for j in range(8):
            which = index_ref[0] if j < 4 else 1 - index_ref[0]
            at = pl.multiple_of(which * 1024 + (j % 4) * 256, 256)
            blocks = []
            for k in range(2):
                place = 2 * (j % 4) + k
                block = own_ref[place, :tokens] if j < 4 else other_ref[place, :tokens]
                column = (iota((tokens, lanes), 1) + (index_ref[1] + at + k * lanes)).astype(f32)
                hit = jnp.where(column == target_ref[...], hits_ref[...], 0.0)
                blocks.append((block.astype(f32) * scales[...] - hit).astype(bf16))
            product = jnp.dot(
                h_ref[...], jnp.concatenate(blocks, axis=1), preferred_element_type=f32
            )
            gw_ref[:, pl.ds(at, 256)] = product.astype(bf16)

    return call(
        kernel,
        [
            jax.ShapeDtypeStruct((depth, tokens), bf16),
            jax.ShapeDtypeStruct((depth, 2048), bf16),
            jax.ShapeDtypeStruct((1, share), f32),
        ],
        [smem] + [vmem] * 6,
        [pltpu.VMEM((tokens, lanes), f32), pltpu.VMEM((tokens + 32, lanes), f32)],
    )(index, reduced, own, other, hits, target, hidden_t)


def per_device(hidden, head_weight, targets, lse_rest, cotangent):
    x, y, z, core = (lax.axis_index(a).astype(jnp.int32) for a in ("x", "y", "z", "core"))
    swap = [(0, 1), (1, 0)]
    vocab = ("x", "y")
    shard = x * 8 + y
    index = jnp.stack([core, shard * 2048, z * 2 + core, shard])
    hidden_t, weight_t = hidden.T, head_weight.T
    vectors = [v.reshape(1, tokens) for v in (targets, lse_rest, cotangent)]

    (sent,) = half_logits(index, hidden_t, weight_t)
    received = lax.ppermute(sent, "core", swap)
    kept, target, small = half_logits(index, hidden_t, weight_t, vectors)
    parts = lax.all_to_all(add_halves(kept, received), "z", 0, 0, tiled=True)
    own = lax.all_to_all(soften(index, parts, target), "z", 0, 0, tiled=True)
    other = lax.ppermute(own, "core", swap)
    before = half_grad(index, own, target, small, weight_t)
    part, hits = half_grad(index, other, target, small, weight_t, before)
    shares = lax.all_to_all(part, vocab, 0, 0, tiled=True)
    spread = reduce_chunk(index, shares, small, hidden.shape[1])
    reduced = lax.all_to_all(spread, vocab, 0, 0, tiled=True)
    grad_hidden, grad_weight, token_loss = finish(
        index, reduced, own, other, hits, target, hidden_t
    )
    return (grad_hidden.T, grad_weight.T, token_loss.reshape(-1))


def solution(mesh):
    mesh = Mesh(mesh.devices.reshape(4, 8, 8, 2), ("x", "y", "z", "core"))
    vocab, width = ("x", "y"), ("z", "core")
    return jax.shard_map(
        per_device,
        mesh=mesh,
        in_specs=(P(None, width), P(vocab, width), P(), P(), P()),
        out_specs=(P(None, width), P(vocab, width), P(width)),
        check_vma=False,
    )
```

time: 144 us -> 138 us (0.958)
  blocking collectives: 49.1 us -> 115 us
  waiting for transfers between devices: 54 us -> 0.88 us
  starting transfers between devices: 24.6 us -> 3.82 us
  Pallas kernels: 10.5 us -> 16.2 us
  local copies, waits for them, and re-layouts: 4.12 us -> 0.03 us
    all_to_all x1 -> x3, blocking collectives: 29.6 us -> 95.6 us  [the longest x1 36.5 us: per_device(): parts = lax.all_to_all(add_halves(kept, received), 'z', 0, 0, tiled=True)]
    all_to_all x2 -> x0, waiting for transfers between devices: 49.1 us -> none  [the longest x1 26.1 us: per_device(): parts = lax.all_to_all(mine, 'z', 0, 0, tiled=True)]
    all_to_all x2 -> x0, starting transfers between devices: 20.7 us -> none  [the longest x1 10.4 us: per_device(): parts = lax.all_to_all(mine, 'z', 0, 0, tiled=True)]
    pallas_call x5 -> x7, Pallas kernels: 7.39 us -> 13.4 us  [the longest x2 7.21 us: half_logits(): pl.pallas_call(kernel, grid_spec=pltpu.PrefetchScalarGridSpec(num_scalar_...]
    unnamed x20 -> x12, local copies, waits for them, and re-layouts: 3.82 us -> 0.03 us
    ppermute x1, waiting for transfers between devices: 2.44 us -> 0.25 us  [per_device(): received = lax.ppermute(sent, 'core', swap)]
    ppermute x1, waiting for transfers between devices: 2.46 us -> 0.64 us  [per_device(): other = lax.ppermute(own, 'core', swap)]
  transfers between devices with their start and end apart: 4 -> 2, of which waited for: 4 -> 2; matrix products, arithmetic and copies ran while one was open for 0% -> 0% of each run, Pallas kernels for 0% -> 3%
where the time goes in v3:
time: 138 us; the launch traced here: 137 us
  blocking collectives  115 us (83%)
  Pallas kernels  16.2 us (12%)
  starting transfers between devices  3.82 us (3%)
    all_to_all x1, blocking collectives, per_device(): parts = lax.all_to_all(add_halves(kept, received), 'z', 0, 0, tiled=True)  36.5 us
    all_to_all x1, blocking collectives, per_device(): shares = lax.all_to_all(part, vocab, 0, 0, tiled=True)  30.6 us
    all_to_all x1, blocking collectives, per_device(): own = lax.all_to_all(soften(index, parts, target), 'z', 0, 0, tiled=True)  28.6 us
    all_to_all x1, blocking collectives, per_device(): reduced = lax.all_to_all(spread, vocab, 0, 0, tiled=True)  19.5 us
    pallas_call x2, Pallas kernels, half_logits(): pl.pallas_call(kernel, grid_spec=pltpu.PrefetchScalarGridSpec(num_scalar_...  7.21 us
    pallas_call x2, Pallas kernels, half_grad(): call(inside, out, [smem] + [vmem] * (4 + len(before)), scratch)  3.84 us
    pallas_call x1, Pallas kernels, finish(): call(kernel, [jax.ShapeDtypeStruct((depth, tokens), bf16), jax.ShapeDtype...  2.81 us
  transfers between devices with their start and end apart: 2, of which 2 were waited for; matrix products, arithmetic and copies ran while one was open for 0% of the time, Pallas kernels for 3%

profile of v3, /device:TPU:8, one launch (start us, length us, event | category | flops | bytes accessed | tf_op | source)
XLA Modules:
  0.0 137.4 jit_solution(16763789380467267724)
XLA Ops:
  0.6 0.0 copy-start
  0.6 0.0 copy-start.1
  0.7 0.0 copy-start.5
  0.7 0.0 copy-start.4
  0.7 0.0 copy-start.3
  0.7 0.6 pad_add_fusion.index_ref.refs_0_
  1.3 0.0 copy-start.2
  1.3 4.9 %shard_map.77 = bf16[8,448,128]{2,1,0:T(8,128)(2,1)} custom-call(s32[4]{0:T(128)} %pad_add_fusion.index_ref.refs_0_, bf16[288,448]{1,0:T(8,128)(2,1)} %bitcast.16, bf16[288,2048]{1,0:T(8,128)(2,1)} %bitcast.12), custom_call_target="tpu_custom_call" | custom-call | tf_op jit(solution)/shard_map/pallas_call | solution.py:91
  6.2 1.9 %collective-permute-start = (bf16[8,448,128]{2,1,0:T(8,128)(2,1)}, bf16[8,448,128]{2,1,0:T(8,128)(2,1)S(1)}, u32[]{:S(2)}, u32[]{:S(2)}) collective-permute-start(bf16[8,448,128]{2,1,0:T(8,128)(2,1)} %shard_map.77), channel_id=1, source_target_pairs={{0,1},{1,0},{2,3},{3,2},{4,5},{5,4},{6,7},{7,6},{8,9},{9,8},{10,11... | collective-permute-start | bytes 2752520 | tf_op jit(solution)/shard_map/ppermute | solution.py:305
  8.1 0.0 copy-done
  8.1 0.0 copy-done.1
  8.1 0.0 copy-done.5
  8.1 0.0 copy-done.4
  8.1 0.0 copy-done.3
  8.1 0.0 copy-done.2
  8.2 2.3 %shard_map.76 = (f32[8,448,128]{2,1,0:T(8,128)S(1)}, f32[448,128]{1,0:T(8,128)S(1)}, f32[512,128]{1,0:T(8,128)S(1)}) custom-call(s32[4]{0:T(128)S(1)} %copy-done.2, bf16[288,448]{1,0:T(8,128)(2,1)S(1)} %bitcast.17, bf16[288,2048]{1,0:T(8,128)(2,1)S(1)} %bitcast.13, s32[1,448]{1,0:T(1,128)S(1)} %bitcast.19, f32[1,448]{1,0:T(1,128)S(1)} %bitcast.20, ...), custom_call_target="tpu_custom_call" | custom-call | tf_op jit(solution)/shard_map/pallas_call | solution.py:91
  10.5 0.2 collective-permute-done.received_ref
  10.7 0.2 shard_map.78
  10.9 36.5 %all_to_all.20.parts_ref = bf16[8,448,128]{2,1,0:T(8,128)(2,1)S(1)} all-to-all(bf16[8,448,128]{2,1,0:T(8,128)(2,1)S(1)} %shard_map.78), channel_id=1, replica_groups=mesh['x'=4,'y'=8,'z'=8,'core'=2] {'z'}, dimensions={0} | all-to-all | bytes 1835008 | tf_op jit(solution)/shard_map/all_to_all | solution.py:307
  47.4 1.3 shard_map.79
  48.7 28.6 %all_to_all.21.refs_1_.own_ref = bf16[8,464,128]{2,1,0:T(8,128)(2,1)S(1)} all-to-all(bf16[8,464,128]{2,1,0:T(8,128)(2,1)S(1)} %shard_map.79), channel_id=1, replica_groups=mesh['x'=4,'y'=8,'z'=8,'core'=2] {'z'}, dimensions={0} | all-to-all | bytes 1900544 | tf_op jit(solution)/shard_map/all_to_all | solution.py:308
  77.3 1.9 %collective-permute-start.1 = (bf16[8,464,128]{2,1,0:T(8,128)(2,1)S(1)}, bf16[8,464,128]{2,1,0:T(8,128)(2,1)S(1)}, u32[]{:S(2)}, u32[]{:S(2)}) collective-permute-start(bf16[8,464,128]{2,1,0:T(8,128)(2,1)S(1)} %all_to_all.21.refs_1_.own_ref), channel_id=1, source_target_pairs={{0,1},{1,0},{2,3},{3,2},{4,5},{5,4},{6,7},{7,6},{8,9},{9,8},{10,11... | collective-permute-start | bytes 2850824 | tf_op jit(solution)/shard_map/ppermute | solution.py:309
  79.2 1.8 %shard_map.80 = (f32[896,288]{1,0:T(8,128)S(1)}, f32[16,128]{1,0:T(8,128)S(1)}) custom-call(s32[4]{0:T(128)S(1)} %copy-done.2, bf16[8,464,128]{2,1,0:T(8,128)(2,1)S(1)} %all_to_all.21.refs_1_.own_ref, f32[448,128]{1,0:T(8,128)S(1)} %get-tuple-element.14.target_ref.refs_2_, f32[512,128]{1,0:T(8,128)S(1)} %get-tuple-element.15.refs_3_.small_ref, ...), custom_call_target="tpu_custom_call" | custom-call | tf_op jit(solution)/shard_map/pallas_call | solution.py:220
  81.0 0.6 collective-permute-done.1.soft_ref.other_ref
  81.7 2.0 %shard_map.81 = (bf16[32,16,640]{2,1,0:T(8,128)(2,1)S(1)}, f32[448,128]{1,0:T(8,128)S(1)}) custom-call(s32[4]{0:T(128)S(1)} %copy-done.2, bf16[8,464,128]{2,1,0:T(8,128)(2,1)S(1)} %collective-permute-done.1.soft_ref.other_ref, f32[448,128]{1,0:T(8,128)S(1)} %get-tuple-element.14.target_ref.refs_2_, f32[512,128]{1,0:T(8,128)S(1)} %get-tuple-element.15.refs_3_.small_ref, ...), custom_call_target="tpu_custom_call" | custom-call | tf_op jit(solution)/shard_map/pallas_call | solution.py:220
  83.7 30.6 %all_to_all.22.parts_ref = bf16[32,16,640]{2,1,0:T(8,128)(2,1)S(1)} all-to-all(bf16[32,16,640]{2,1,0:T(8,128)(2,1)S(1)} %get-tuple-element.18), channel_id=1, replica_groups=mesh['x'=4,'y'=8,'z'=8,'core'=2] {'x','y'}, dimensions={0} | all-to-all | bytes 1310720 | tf_op jit(solution)/shard_map/all_to_all | solution.py:312
  114.3 0.8 shard_map.82
  115.1 19.5 %all_to_all.23.reduced_ref = bf16[32,16,384]{2,1,0:T(8,128)(2,1)S(1)} all-to-all(bf16[32,16,384]{2,1,0:T(8,128)(2,1)S(1)} %shard_map.82), channel_id=1, replica_groups=mesh['x'=4,'y'=8,'z'=8,'core'=2] {'x','y'}, dimensions={0} | all-to-all | bytes 786432 | tf_op jit(solution)/shard_map/all_to_all | solution.py:314
  134.6 2.8 %shard_map.83 = (bf16[288,448]{1,0:T(8,128)(2,1)}, bf16[288,2048]{1,0:T(8,128)(2,1)}, f32[1,28]{1,0:T(1,128)}) custom-call(s32[4]{0:T(128)S(1)} %copy-done.2, bf16[32,16,384]{2,1,0:T(8,128)(2,1)S(1)} %all_to_all.23.reduced_ref, bf16[8,464,128]{2,1,0:T(8,128)(2,1)S(1)} %all_to_all.21.refs_1_.own_ref, ...), custom_call_target="tpu_custom_call" | custom-call | tf_op jit(solution)/shard_map/pallas_call | solution.py:283
Async XLA Ops:
  0.6 7.5 %copy-start = (bf16[2048,288]{0,1:T(8,128)(2,1)S(1)}, bf16[2048,288]{0,1:T(8,128)(2,1)}, u32[]{:S(2)}) copy-start(bf16[2048,288]{0,1:T(8,128)(2,1)} %param.6) | copy-start | bytes 3538948
  0.6 7.5 %copy-start.1 = (bf16[448,288]{0,1:T(8,128)(2,1)S(1)}, bf16[448,288]{0,1:T(8,128)(2,1)}, u32[]{:S(2)}) copy-start(bf16[448,288]{0,1:T(8,128)(2,1)} %param.5) | copy-start | bytes 774148
  0.7 7.5 %copy-start.5 = (f32[448]{0:T(512)S(1)}, f32[448]{0:T(512)}, u32[]{:S(2)}) copy-start(f32[448]{0:T(512)} %param.9) | copy-start | bytes 5380
  0.7 7.5 %copy-start.4 = (f32[448]{0:T(512)S(1)}, f32[448]{0:T(512)}, u32[]{:S(2)}) copy-start(f32[448]{0:T(512)} %param.8) | copy-start | bytes 5380
  0.7 7.5 %copy-start.3 = (s32[448]{0:T(512)S(1)}, s32[448]{0:T(512)}, u32[]{:S(2)}) copy-start(s32[448]{0:T(512)} %param.7) | copy-start | bytes 5380
  1.3 6.8 %copy-start.2 = (s32[4]{0:T(128)S(1)}, s32[4]{0:T(128)}, u32[]{:S(2)}) copy-start(s32[4]{0:T(128)} %pad_add_fusion.index_ref.refs_0_) | copy-start | bytes 52
  6.2 4.6 %collective-permute-start = (bf16[8,448,128]{2,1,0:T(8,128)(2,1)}, bf16[8,448,128]{2,1,0:T(8,128)(2,1)S(1)}, u32[]{:S(2)}, u32[]{:S(2)}) collective-permute-start(bf16[8,448,128]{2,1,0:T(8,128)(2,1)} %shard_map.77), channel_id=1, source_target_pairs={{0,1},{1,0},{2,3},{3,2},{4,5},{5,4},{6,7},{7,6},{8,9},{9,8},{10,11... | collective-permute-start | bytes 2752520 | tf_op jit(solution)/shard_map/ppermute | solution.py:305
  77.3 4.4 %collective-permute-start.1 = (bf16[8,464,128]{2,1,0:T(8,128)(2,1)S(1)}, bf16[8,464,128]{2,1,0:T(8,128)(2,1)S(1)}, u32[]{:S(2)}, u32[]{:S(2)}) collective-permute-start(bf16[8,464,128]{2,1,0:T(8,128)(2,1)S(1)} %all_to_all.21.refs_1_.own_ref), channel_id=1, source_target_pairs={{0,1},{1,0},{2,3},{3,2},{4,5},{5,4},{6,7},{7,6},{8,9},{9,8},{10,11... | collective-permute-start | bytes 2850824 | tf_op jit(solution)/shard_map/ppermute | solution.py:309

commit v4 on v3

--- a/solution.py
+++ b/solution.py
@@ -17,6 +17,7 @@
 bf16, f32 = jnp.bfloat16, jnp.float32
 vmem = pl.BlockSpec(memory_space=pltpu.VMEM)
 smem = pl.BlockSpec(memory_space=pltpu.SMEM)
+hbm = pl.BlockSpec(memory_space=pltpu.HBM)
 
 
 def call(kernel, out_shape, in_specs, scratch=()):
@@ -50,57 +51,60 @@
     return out
 
 
-def half_logits(index, hidden_t, weight_t, vectors=()):
+def sent_logits(index, hidden_t, weight_t):
     depth = hidden_t.shape[0]
-    own = bool(vectors)
-    kind = f32 if own else bf16
-
-    def kernel(index_ref, h_ref, w_ref, *refs):
-        turned = refs[-1]
-        out_ref = refs[3] if own else refs[0]
-
-        @pl.when(pl.program_id(0) == 0)
-        def _():
-            turned[...] = jnp.transpose(h_ref[...])
-            if own:
-                target_ref, rest_ref, cot_ref = refs[:3]
-                rows = rows_of(target_ref[...].astype(f32)) + rows_of(rest_ref[...]) + rows_of(cot_ref[...])
-                tile = jnp.zeros((16, lanes), f32)
-                for r, row in enumerate(rows):
-                    tile = jnp.where(iota((16, lanes), 0) == r, row, tile)
-                target, rest, cot, _ = columns_of(tile)
-                refs[4][...] = target
-                refs[5][:tokens] = jnp.where(iota((tokens, lanes), 1) == 0, rest, cot)
-                refs[5][tokens:] = jnp.zeros((shards * chunk - tokens, lanes), f32)
-
-        part = jnp.dot(turned[...], w_ref[...], preferred_element_type=f32).astype(kind)
-        out_ref[0] = part[:, :lanes]
-        out_ref[1] = part[:, lanes:]
-
-    def whole(*shape):
-        return pl.BlockSpec(shape, lambda i, c: (0,) * len(shape))
-
-    def block(i, c):
-        return (0, (c[0] if own else 1 - c[0]) * 4 + i)
-
-    out_specs = [pl.BlockSpec((2, tokens, lanes), lambda i, c: (i, 0, 0))]
-    out_shape = [jax.ShapeDtypeStruct((8, tokens, lanes), kind)]
-    if own:
-        out_specs += [whole(tokens, lanes), whole(shards * chunk, lanes)]
-        out_shape += [jax.ShapeDtypeStruct(spec.block_shape, f32) for spec in out_specs[1:]]
+
+    def kernel(index_ref, h_hbm, w_hbm, out_ref, h_ref, w_ref, arrived):
+        half = pl.multiple_of((1 - index_ref[0]) * 1024, 1024)
+        first = pltpu.make_async_copy(h_hbm, h_ref, arrived.at[0])
+        second = pltpu.make_async_copy(w_hbm.at[:, pl.ds(half, 1024)], w_ref, arrived.at[1])
+        first.start()
+        second.start()
+        first.wait()
+        h = jnp.transpose(h_ref[...])
+        second.wait()
+        for i in range(4):
+            part = jnp.dot(h, w_ref[:, i * 256 : (i + 1) * 256], preferred_element_type=f32)
+            out_ref[2 * i] = part[:, :lanes].astype(bf16)
+            out_ref[2 * i + 1] = part[:, lanes:].astype(bf16)
+
     return pl.pallas_call(
         kernel,
-        grid_spec=pltpu.PrefetchScalarGridSpec(
-            num_scalar_prefetch=1,
-            grid=(4,),
-            in_specs=[whole(depth, tokens), pl.BlockSpec((depth, 256), block)]
-            + [whole(1, tokens)] * len(vectors),
-            out_specs=out_specs,
-            scratch_shapes=[pltpu.VMEM((tokens, depth), bf16)],
-        ),
-        out_shape=out_shape,
-        compiler_params=pltpu.CompilerParams(vmem_limit_bytes=(32 if own else 60) * 1024 * 1024),
-    )(index, hidden_t, weight_t, *vectors)
+        in_specs=[smem, hbm, hbm],
+        out_specs=vmem,
+        out_shape=jax.ShapeDtypeStruct((8, tokens, lanes), bf16),
+        scratch_shapes=[
+            pltpu.VMEM((depth, tokens), bf16),
+            pltpu.VMEM((depth, 1024), bf16),
+            pltpu.SemaphoreType.DMA((2,)),
+        ],
+        compiler_params=pltpu.CompilerParams(vmem_limit_bytes=60 * 1024 * 1024),
+    )(index, hidden_t, weight_t)
+
+
+def kept_logits(index, hidden_t, weight_t, vectors):
+    def kernel(index_ref, h_ref, w_ref, target_ref, rest_ref, cot_ref, out_ref, wanted_ref, small_ref):
+        rows = rows_of(target_ref[...].astype(f32)) + rows_of(rest_ref[...]) + rows_of(cot_ref[...])
+        tile = jnp.zeros((16, lanes), f32)
+        for r, row in enumerate(rows):
+            tile = jnp.where(iota((16, lanes), 0) == r, row, tile)
+        target, rest, cot, _ = columns_of(tile)
+        wanted_ref[...] = target
+        small_ref[:tokens] = jnp.where(iota((tokens, lanes), 1) == 0, rest, cot)
+        small_ref[tokens:] = jnp.zeros((shards * chunk - tokens, lanes), f32)
+        h = jnp.transpose(h_ref[...])
+        for i in range(4):
+            at = pl.multiple_of(index_ref[0] * 1024 + i * 256, 256)
+            part = jnp.dot(h, w_ref[:, pl.ds(at, 256)], preferred_element_type=f32)
+            out_ref[2 * i] = part[:, :lanes]
+            out_ref[2 * i + 1] = part[:, lanes:]
+
+    out = [
+        jax.ShapeDtypeStruct((8, tokens, lanes), f32),
+        jax.ShapeDtypeStruct((tokens, lanes), f32),
+        jax.ShapeDtypeStruct((shards * chunk, lanes), f32),
+    ]
+    return call(kernel, out, [smem] + [vmem] * 5)(index, hidden_t, weight_t, *vectors)
 
 
 def add_halves(kept, received):
@@ -126,7 +130,7 @@
         power = jnp.exp(capped - soft_cap)
         soft = (power * (1.0 - ratio * ratio)).astype(bf16)
         first = index_ref[1] + index_ref[0] * 1024 + (index_ref[2] // 2) * lanes
-        columns = (iota((tokens, lanes), 1) + first).astype(f32)
+        columns = (iota((1, lanes), 1) + first).astype(f32)
         hit = jnp.where(columns == target_ref[...], capped, 0.0)
 
         def total(block):
@@ -146,11 +150,10 @@
                 tile = jnp.where(row == 8 * k + r, high, tile)
                 tile = jnp.where(row == 8 * k + 4 + r, low, tile)
         tile = tile.astype(bf16)
-        for i in range(8):
-            out_ref[i, :tokens] = soft
-            out_ref[i, tokens:] = tile
-
-    out = jax.ShapeDtypeStruct((8, tokens + chunk, lanes), bf16)
+        out_ref[:filled] = soft.reshape(filled, chunk, lanes)
+        out_ref[filled] = tile
+
+    out = jax.ShapeDtypeStruct((filled + 1, chunk, lanes), bf16)
     return call(kernel, out, [smem, vmem, vmem])(index, parts, target)
 
 
@@ -161,7 +164,7 @@
     def kernel(index_ref, soft_ref, target_ref, small_ref, w_ref, *refs):
         sums = jnp.zeros((chunk, lanes), f32)
         for i in range(8):
-            sums = sums + soft_ref[i, tokens:].astype(f32)
+            sums = sums + soft_ref[filled, i].astype(f32)
         if last:
             sums = sums + refs[1][...]
         rows = [sums[0:4] + sums[4:8], sums[8:12] + sums[12:16]]
@@ -175,9 +178,10 @@
             at = pl.multiple_of(which * 1024 + j * 256, 256)
             blocks = []
             for k in range(2):
-                column = (iota((tokens, lanes), 1) + (index_ref[1] + at + k * lanes)).astype(f32)
+                column = (iota((1, lanes), 1) + (index_ref[1] + at + k * lanes)).astype(f32)
                 hit = jnp.where(column == target_ref[...], hits, 0.0).astype(bf16)
-                blocks.append(jnp.concatenate([soft_ref[2 * j + k, :tokens], hit], axis=0))
+                soft = soft_ref[:filled, 2 * j + k].reshape(tokens, lanes)
+                blocks.append(jnp.concatenate([soft, hit], axis=0))
             product = lax.dot_general(
                 jnp.concatenate(blocks, axis=1),
                 w_ref[:, pl.ds(at, 256)],
@@ -271,8 +275,8 @@
             blocks = []
             for k in range(2):
                 place = 2 * (j % 4) + k
-                block = own_ref[place, :tokens] if j < 4 else other_ref[place, :tokens]
-                column = (iota((tokens, lanes), 1) + (index_ref[1] + at + k * lanes)).astype(f32)
+                block = (own_ref if j < 4 else other_ref)[:filled, place].reshape(tokens, lanes)
+                column = (iota((1, lanes), 1) + (index_ref[1] + at + k * lanes)).astype(f32)
                 hit = jnp.where(column == target_ref[...], hits_ref[...], 0.0)
                 blocks.append((block.astype(f32) * scales[...] - hit).astype(bf16))
             product = jnp.dot(
@@ -301,11 +305,11 @@
     hidden_t, weight_t = hidden.T, head_weight.T
     vectors = [v.reshape(1, tokens) for v in (targets, lse_rest, cotangent)]
 
-    (sent,) = half_logits(index, hidden_t, weight_t)
-    received = lax.ppermute(sent, "core", swap)
-    kept, target, small = half_logits(index, hidden_t, weight_t, vectors)
-    parts = lax.all_to_all(add_halves(kept, received), "z", 0, 0, tiled=True)
-    own = lax.all_to_all(soften(index, parts, target), "z", 0, 0, tiled=True)
+    received = lax.ppermute(sent_logits(core.reshape(1), hidden_t, weight_t), "core", swap)
+    kept, target, small = kept_logits(index, hidden_t, weight_t, vectors)
+    parts = add_halves(kept, received)
+    parts = lax.all_to_all(parts, "z", 0, 0, tiled=True)
+    own = lax.all_gather(soften(index, parts, target), "z", axis=1)
     other = lax.ppermute(own, "core", swap)
     before = half_grad(index, own, target, small, weight_t)
     part, hits = half_grad(index, other, target, small, weight_t, before)

time: 138 us -> 133 us (0.964)
  Pallas kernels: 16.2 us -> 13.1 us
  blocking collectives: 115 us -> 113 us
    all_to_all x2 -> x1, blocking collectives: 65 us -> 36.3 us  [per_device(): parts = lax.all_to_all(parts, 'z', 0, 0, tiled=True)]
    all_gather x0 -> x1, blocking collectives: none -> 26.2 us  [per_device(): own = lax.all_gather(soften(index, parts, target), 'z', axis=1)]
    pallas_call x2, Pallas kernels: 7.21 us -> 4.08 us  [the longest x1 2.83 us: sent_logits(): pl.pallas_call(kernel, in_specs=[smem, hbm, hbm], out_specs=vmem, out_sha...]
  transfers between devices with their start and end apart: 2 -> 2, of which waited for: 2 -> 2; matrix products, arithmetic and copies ran while one was open for 0% -> 0% of each run, Pallas kernels for 3% -> 2%
where the time goes in v4:
time: 133 us; the launch traced here: 132 us
  blocking collectives  113 us (85%)
  Pallas kernels  13.1 us (10%)
  starting transfers between devices  3.83 us (3%)
  waiting for transfers between devices  1.9 us (1%)
    all_to_all x1, blocking collectives, per_device(): parts = lax.all_to_all(parts, 'z', 0, 0, tiled=True)  36.3 us
    all_to_all x1, blocking collectives, per_device(): shares = lax.all_to_all(part, vocab, 0, 0, tiled=True)  30.6 us
    all_gather x1, blocking collectives, per_device(): own = lax.all_gather(soften(index, parts, target), 'z', axis=1)  26.2 us
    all_to_all x1, blocking collectives, per_device(): reduced = lax.all_to_all(spread, vocab, 0, 0, tiled=True)  19.5 us
    pallas_call x2, Pallas kernels, half_grad(): call(inside, out, [smem] + [vmem] * (4 + len(before)), scratch)  3.87 us
    pallas_call x1, Pallas kernels, finish(): call(kernel, [jax.ShapeDtypeStruct((depth, tokens), bf16), jax.ShapeDtype...  2.85 us
    pallas_call x1, Pallas kernels, sent_logits(): pl.pallas_call(kernel, in_specs=[smem, hbm, hbm], out_specs=vmem, out_sha...  2.83 us
  transfers between devices with their start and end apart: 2, of which 2 were waited for; matrix products, arithmetic and copies ran while one was open for 0% of the time, Pallas kernels for 2%

profile of v4, /device:TPU:8, one launch (start us, length us, event | category | flops | bytes accessed | tf_op | source)
XLA Modules:
  0.0 132.3 jit_solution(13060961208235635620)
XLA Ops:
  0.6 0.0 copy-start
  0.6 0.0 copy-start.1
  0.7 0.0 copy-start.4
  0.7 0.0 copy-start.3
  0.7 0.0 copy-start.2
  0.7 2.8 %shard_map.77 = bf16[8,448,128]{2,1,0:T(8,128)(2,1)} custom-call(s32[1]{0:T(128)} %bitcast.index_ref, bf16[288,448]{1,0:T(8,128)(2,1)} %bitcast.20, bf16[288,2048]{1,0:T(8,128)(2,1)} %bitcast.13), custom_call_target="tpu_custom_call" | custom-call | tf_op jit(solution)/shard_map/pallas_call | solution.py:71
  3.5 1.9 %collective-permute-start = (bf16[8,448,128]{2,1,0:T(8,128)(2,1)}, bf16[8,448,128]{2,1,0:T(8,128)(2,1)S(1)}, u32[]{:S(2)}, u32[]{:S(2)}) collective-permute-start(bf16[8,448,128]{2,1,0:T(8,128)(2,1)} %shard_map.77), channel_id=1, source_target_pairs={{0,1},{1,0},{2,3},{3,2},{4,5},{5,4},{6,7},{7,6},{8,9},{9,8},{10,11... | collective-permute-start | bytes 2752520 | tf_op jit(solution)/shard_map/ppermute | solution.py:308
  5.5 0.1 pad_add_fusion.index_ref.refs_0_
  5.5 0.0 copy-done
  5.5 0.0 copy-done.1
  5.5 0.0 copy-done.4
  5.6 0.0 copy-done.3
  5.6 0.0 copy-done.2
  5.6 1.2 shard_map.76
  6.8 1.3 collective-permute-done.received_ref
  8.1 0.2 shard_map.78
  8.3 36.3 %all_to_all.15.parts_ref = bf16[8,448,128]{2,1,0:T(8,128)(2,1)S(1)} all-to-all(bf16[8,448,128]{2,1,0:T(8,128)(2,1)S(1)} %shard_map.78), channel_id=1, replica_groups=mesh['x'=4,'y'=8,'z'=8,'core'=2] {'z'}, dimensions={0} | all-to-all | bytes 1835008 | tf_op jit(solution)/shard_map/all_to_all | solution.py:311
  44.6 1.3 %shard_map.79 = bf16[29,16,128]{2,1,0:T(8,128)(2,1)S(1)} custom-call(s32[4]{0:T(128)S(1)} %pad_add_fusion.index_ref.refs_0_, bf16[8,448,128]{2,1,0:T(8,128)(2,1)S(1)} %all_to_all.15.parts_ref, f32[448,128]{1,0:T(8,128)S(1)} %get-tuple-element.14.target_ref.refs_2_), custom_call_target="tpu_custom_call" | custom-call | tf_op jit(solution)/shard_map/pallas_call | solution.py:157
  45.9 26.2 %all-gather = bf16[29,128,128]{2,1,0:T(8,128)(2,1)S(1)} all-gather(bf16[29,16,128]{2,1,0:T(8,128)(2,1)S(1)} %shard_map.79), channel_id=2, replica_groups=mesh['x'=4,'y'=8,'z'=8,'core'=2] {'z'}, dimensions={1}, use_global_device_ids=true | all-gather | bytes 1069056 | tf_op jit(solution)/shard_map/all_gather | solution.py:312
  72.1 1.9 %collective-permute-start.1 = (bf16[29,8,16,128]{3,2,1,0:T(8,128)(2,1)S(1)}, bf16[29,8,16,128]{3,2,1,0:T(8,128)(2,1)S(1)}, u32[]{:S(2)}, u32[]{:S(2)}) collective-permute-start(bf16[29,8,16,128]{3,2,1,0:T(8,128)(2,1)S(1)} %bitcast.17), channel_id=1, source_target_pairs={{0,1},{1,0},{2,3},{3,2},{4,5},{5,4},{6,7},{7,6},{8,9},{9,8},{10,11... | collective-permute-start | bytes 2850824 | tf_op jit(solution)/shard_map/ppermute | solution.py:313
  74.0 1.9 %shard_map.80 = (f32[896,288]{1,0:T(8,128)S(1)}, f32[16,128]{1,0:T(8,128)S(1)}) custom-call(s32[4]{0:T(128)S(1)} %pad_add_fusion.index_ref.refs_0_, bf16[29,8,16,128]{3,2,1,0:T(8,128)(2,1)S(1)} %bitcast.18, f32[448,128]{1,0:T(8,128)S(1)} %get-tuple-element.14.target_ref.refs_2_, f32[512,128]{1,0:T(8,128)S(1)} %get-tuple-element.15.refs_3_.small_ref, ...), custom_call_target="tpu_custom_call" | custom-call | tf_op jit(solution)/shard_map/pallas_call | solution.py:224
  75.9 0.6 collective-permute-done.1.soft_ref.other_ref
  76.5 2.0 %shard_map.81 = (bf16[32,16,640]{2,1,0:T(8,128)(2,1)S(1)}, f32[448,128]{1,0:T(8,128)S(1)}) custom-call(s32[4]{0:T(128)S(1)} %pad_add_fusion.index_ref.refs_0_, bf16[29,8,16,128]{3,2,1,0:T(8,128)(2,1)S(1)} %collective-permute-done.1.soft_ref.other_ref, f32[448,128]{1,0:T(8,128)S(1)} %get-tuple-element.14.target_ref.refs_2_, ...), custom_call_target="tpu_custom_call" | custom-call | tf_op jit(solution)/shard_map/pallas_call | solution.py:224
  78.5 30.6 %all_to_all.16.parts_ref = bf16[32,16,640]{2,1,0:T(8,128)(2,1)S(1)} all-to-all(bf16[32,16,640]{2,1,0:T(8,128)(2,1)S(1)} %get-tuple-element.18), channel_id=1, replica_groups=mesh['x'=4,'y'=8,'z'=8,'core'=2] {'x','y'}, dimensions={0} | all-to-all | bytes 1310720 | tf_op jit(solution)/shard_map/all_to_all | solution.py:316
  109.1 0.8 shard_map.82
  109.9 19.5 %all_to_all.17.reduced_ref = bf16[32,16,384]{2,1,0:T(8,128)(2,1)S(1)} all-to-all(bf16[32,16,384]{2,1,0:T(8,128)(2,1)S(1)} %shard_map.82), channel_id=1, replica_groups=mesh['x'=4,'y'=8,'z'=8,'core'=2] {'x','y'}, dimensions={0} | all-to-all | bytes 786432 | tf_op jit(solution)/shard_map/all_to_all | solution.py:318
  129.4 2.8 %shard_map.83 = (bf16[288,448]{1,0:T(8,128)(2,1)}, bf16[288,2048]{1,0:T(8,128)(2,1)}, f32[1,28]{1,0:T(1,128)}) custom-call(s32[4]{0:T(128)S(1)} %pad_add_fusion.index_ref.refs_0_, bf16[32,16,384]{2,1,0:T(8,128)(2,1)S(1)} %all_to_all.17.reduced_ref, bf16[29,8,16,128]{3,2,1,0:T(8,128)(2,1)S(1)} %bitcast.19, ...), custom_call_target="tpu_custom_call" | custom-call | tf_op jit(solution)/shard_map/pallas_call | solution.py:287
Async XLA Ops:
  0.6 4.9 %copy-start = (bf16[2048,288]{0,1:T(8,128)(2,1)S(1)}, bf16[2048,288]{0,1:T(8,128)(2,1)}, u32[]{:S(2)}) copy-start(bf16[2048,288]{0,1:T(8,128)(2,1)} %param.6) | copy-start | bytes 3538948
  0.6 4.9 %copy-start.1 = (bf16[448,288]{0,1:T(8,128)(2,1)S(1)}, bf16[448,288]{0,1:T(8,128)(2,1)}, u32[]{:S(2)}) copy-start(bf16[448,288]{0,1:T(8,128)(2,1)} %param.5) | copy-start | bytes 774148
  0.7 4.9 %copy-start.4 = (f32[448]{0:T(512)S(1)}, f32[448]{0:T(512)}, u32[]{:S(2)}) copy-start(f32[448]{0:T(512)} %param.9) | copy-start | bytes 5380
  0.7 4.9 %copy-start.3 = (f32[448]{0:T(512)S(1)}, f32[448]{0:T(512)}, u32[]{:S(2)}) copy-start(f32[448]{0:T(512)} %param.8) | copy-start | bytes 5380
  0.7 4.9 %copy-start.2 = (s32[448]{0:T(512)S(1)}, s32[448]{0:T(512)}, u32[]{:S(2)}) copy-start(s32[448]{0:T(512)} %param.7) | copy-start | bytes 5380
  3.5 4.6 %collective-permute-start = (bf16[8,448,128]{2,1,0:T(8,128)(2,1)}, bf16[8,448,128]{2,1,0:T(8,128)(2,1)S(1)}, u32[]{:S(2)}, u32[]{:S(2)}) collective-permute-start(bf16[8,448,128]{2,1,0:T(8,128)(2,1)} %shard_map.77), channel_id=1, source_target_pairs={{0,1},{1,0},{2,3},{3,2},{4,5},{5,4},{6,7},{7,6},{8,9},{9,8},{10,11... | collective-permute-start | bytes 2752520 | tf_op jit(solution)/shard_map/ppermute | solution.py:308
  72.1 4.4 %collective-permute-start.1 = (bf16[29,8,16,128]{3,2,1,0:T(8,128)(2,1)S(1)}, bf16[29,8,16,128]{3,2,1,0:T(8,128)(2,1)S(1)}, u32[]{:S(2)}, u32[]{:S(2)}) collective-permute-start(bf16[29,8,16,128]{3,2,1,0:T(8,128)(2,1)S(1)} %bitcast.17), channel_id=1, source_target_pairs={{0,1},{1,0},{2,3},{3,2},{4,5},{5,4},{6,7},{7,6},{8,9},{9,8},{10,11... | collective-permute-start | bytes 2850824 | tf_op jit(solution)/shard_map/ppermute | solution.py:313

commit v5 on v4

--- a/solution.py
+++ b/solution.py
@@ -12,8 +12,8 @@
 chunk = 16
 shards = 32
 filled = tokens // chunk
-padded = 384
-packed = 640
+share = 14
+tail_rows = 7
 bf16, f32 = jnp.bfloat16, jnp.float32
 vmem = pl.BlockSpec(memory_space=pltpu.VMEM)
 smem = pl.BlockSpec(memory_space=pltpu.SMEM)
@@ -113,6 +113,42 @@
             out_ref[i] = (kept_ref[i] + received_ref[i].astype(f32)).astype(bf16)
 
     return call(kernel, jax.ShapeDtypeStruct(kept.shape, bf16), [vmem, vmem])(kept, received)
+
+
+def places(axis):
+    shape = (shards * chunk, 1) if axis == 0 else (1, shards * chunk)
+    row = iota(shape, axis)
+    number, inside = row // chunk, row % chunk
+    token = jnp.where(inside < share, number * share + inside, -1)
+    group = jnp.where(inside < share, -1, number * 2 + inside - share)
+    return token, group
+
+
+def ones_where(condition):
+    return jnp.where(condition, 1.0, 0.0).astype(bf16)
+
+
+def exact(a, b):
+    wide = a.dtype == f32 or b.dtype == f32
+    precision = lax.Precision.HIGHEST if wide else None
+    return jnp.dot(a, b, precision=precision, preferred_element_type=f32)
+
+
+def repeated(tail, width, lanes_out, member):
+    lane = iota((lanes, lanes_out), 1)
+    spread = (lane % width == iota((lanes, lanes_out), 0)) & (lane < width * tail_rows)
+    slot = iota((1, lanes_out), 1) // width
+    return jnp.where(slot == member, exact(tail, ones_where(spread)), 0.0).astype(bf16)
+
+
+def folded(wide, width, member):
+    lanes_in = wide.shape[1]
+    lane = iota((lanes_in, lanes), 0)
+    fold = (lane % width == iota((lanes_in, lanes), 1)) & (lane < width * tail_rows)
+    slot = iota((1, lanes_in), 1) // width
+    mine = jnp.where(slot == member, wide, 0.0)
+    fold = jnp.where(fold, 1.0, 0.0)
+    return exact(mine, fold) if mine.dtype == f32 else exact(mine, fold.astype(bf16))
 
 
 def high_low(tile):
@@ -201,18 +237,21 @@
         hits_ref[...] = hits
         first, second = total[:tokens], total[tokens:]
         lane = iota((tokens, lanes), 1)
-        end = jnp.concatenate([second[:, 224:], jnp.zeros((tokens, lanes - depth + 224), f32)], axis=1)
+        tail = jnp.concatenate([second[:, 224:], jnp.zeros((tokens, lanes - depth + 224), f32)], axis=1)
         for k, column in enumerate(high_low(power) + high_low(picked)):
-            end = jnp.where(lane == depth - 224 + k, column, end)
-        middle = jnp.concatenate([first[:, 256:], second[:, :96]], axis=1)
-        for t, piece in enumerate((first[:, :lanes], first[:, lanes:256], middle, second[:, 96:224], end)):
-            out_ref[:filled, :, t * lanes : (t + 1) * lanes] = piece.astype(bf16).reshape(filled, chunk, lanes)
-        out_ref[filled:] = jnp.zeros((shards - filled, chunk, packed), bf16)
+            tail = jnp.where(lane == depth - 224 + k, column, tail)
+        tail = repeated(tail.astype(bf16), depth - 220, 512, iota((tokens, 1), 0) % tail_rows)
+        main = jnp.concatenate([first, second[:, :224]], axis=1).astype(bf16)
+        token, group = places(0)
+        each = iota((1, tokens), 1)
+        choose = [ones_where(token == each), ones_where(group == each // tail_rows)]
+        out = exact(jnp.concatenate(choose, axis=1), jnp.concatenate([main, tail], axis=0))
+        out_ref[...] = out.astype(bf16).reshape(shards, chunk, 512)
 
     total = (2 * tokens, depth)
     if last:
         out = [
-            jax.ShapeDtypeStruct((shards, chunk, packed), bf16),
+            jax.ShapeDtypeStruct((shards, chunk, 512), bf16),
             jax.ShapeDtypeStruct((tokens, lanes), f32),
         ]
         scratch = [pltpu.VMEM(total, f32)]
@@ -231,44 +270,55 @@
         total = parts_ref[0].astype(f32)
         for i in range(1, shards):
             total = total + parts_ref[i].astype(f32)
-        mine = small_ref[pl.ds(pl.multiple_of(index_ref[3] * chunk, chunk), chunk)]
+        mine = small_ref[pl.ds(index_ref[3] * share, chunk)]
         rest, cot = mine[:, 0:1], mine[:, 1:2]
-        at = 2 * depth
-        power = total[:, at : at + 1] + total[:, at + 1 : at + 2]
-        picked = total[:, at + 2 : at + 3] + total[:, at + 3 : at + 4]
+        row, column = iota((chunk, 1), 0), iota((1, chunk), 1)
+        own = (column == share + row // tail_rows) & (row < share)
+        held = exact(jnp.where(own, 1.0, 0.0), total)
+        tail = folded(held, depth - 220, row % tail_rows)
+        at = depth - 224
+        power = tail[:, at : at + 1] + tail[:, at + 1 : at + 2]
+        picked = tail[:, at + 2 : at + 3] + tail[:, at + 3 : at + 4]
         slab = jnp.log(power) + soft_cap
         larger, smaller = jnp.maximum(slab, rest), jnp.minimum(slab, rest)
         lse = larger + jnp.log(1.0 + jnp.exp(smaller - larger))
         loss = lse - picked + zloss_weight * lse * lse
         scale = cot * (1.0 + 2.0 * zloss_weight * lse) * jnp.exp(soft_cap - lse)
-        out = total[:, :depth] * scale - total[:, depth:at]
-        out = jnp.concatenate([out, jnp.zeros((chunk, padded - depth), f32)], axis=1)
-        lane = iota((chunk, padded), 1)
-        for k, column in enumerate(high_low(scale) + high_low(loss)):
-            out = jnp.where(lane == depth + k, column, out)
-        out = out.astype(bf16)
+        second = jnp.concatenate([total[:, depth:], tail[:, :at]], axis=1)
+        out = jnp.where(row < share, total[:, :depth] * scale - second, 0.0)
+        end = jnp.concatenate([out[:, 256:], jnp.zeros((chunk, lanes - depth + 256), f32)], axis=1)
+        lane = iota((chunk, lanes), 1)
+        for k, column_k in enumerate(high_low(scale) + high_low(loss)):
+            end = jnp.where((lane == depth - 256 + k) & (row < share), column_k, end)
+        end = repeated(end.astype(bf16), depth - 252, 256, row % tail_rows)
+        into = ones_where((row == share + column // tail_rows) & (column < share))
+        out = (out[:, :256] + exact(into, end)).astype(bf16)
         for i in range(shards):
             out_ref[i] = out
 
-    out = jax.ShapeDtypeStruct((shards, chunk, padded), bf16)
+    out = jax.ShapeDtypeStruct((shards, chunk, 256), bf16)
     return call(kernel, out, [smem, vmem, vmem])(index, parts, small)
 
 
 def finish(index, reduced, own, other, hits, target, hidden_t):
     depth = hidden_t.shape[0]
-    share = tokens // 16
+    losses_each = tokens // 16
 
     def kernel(
         index_ref, reduced_ref, own_ref, other_ref, hits_ref, target_ref, h_ref,
         gh_ref, gw_ref, loss_ref, scales, losses,
     ):
-        last = reduced_ref[:filled, :, 256:].reshape(tokens, lanes).astype(f32)
+        token, group = places(1)
+        each = iota((tokens, 1), 0)
+        choose = [ones_where(token == each), ones_where(group == each // tail_rows)]
+        held = exact(jnp.concatenate(choose, axis=0), reduced_ref[...].reshape(shards * chunk, 256))
+        last = folded(held[tokens:].astype(bf16), depth - 252, each % tail_rows)
         at = depth - 256
         scales[...] = jnp.broadcast_to(last[:, at : at + 1] + last[:, at + 1 : at + 2], (tokens, lanes))
         losses[:tokens] = jnp.broadcast_to(last[:, at + 2 : at + 3] + last[:, at + 3 : at + 4], (tokens, lanes))
-        loss_ref[...] = jnp.transpose(losses[pl.ds(index_ref[2] * share, 32)])[0:1, :share]
-        summed = reduced_ref[:filled].reshape(tokens, padded).astype(f32)
-        gh_ref[...] = jnp.transpose(summed)[:depth].astype(bf16)
+        loss_ref[...] = jnp.transpose(losses[pl.ds(index_ref[2] * losses_each, 32)])[0:1, :losses_each]
+        gh_ref[:256] = jnp.transpose(held[:tokens]).astype(bf16)
+        gh_ref[256:] = jnp.transpose(last)[:at].astype(bf16)
         for j in range(8):
             which = index_ref[0] if j < 4 else 1 - index_ref[0]
             at = pl.multiple_of(which * 1024 + (j % 4) * 256, 256)
@@ -289,7 +339,7 @@
         [
             jax.ShapeDtypeStruct((depth, tokens), bf16),
             jax.ShapeDtypeStruct((depth, 2048), bf16),
-            jax.ShapeDtypeStruct((1, share), f32),
+            jax.ShapeDtypeStruct((1, losses_each), f32),
         ],
         [smem] + [vmem] * 6,
         [pltpu.VMEM((tokens, lanes), f32), pltpu.VMEM((tokens + 32, lanes), f32)],

time: 133 us -> 129 us (0.970)
  blocking collectives: 113 us -> 107 us
  Pallas kernels: 13.1 us -> 15.3 us
    all_to_all x1, blocking collectives: 19.5 us -> 16.7 us  [per_device(): reduced = lax.all_to_all(spread, vocab, 0, 0, tiled=True)]
    all_to_all x1, blocking collectives: 30.6 us -> 27.9 us  [per_device(): shares = lax.all_to_all(part, vocab, 0, 0, tiled=True)]
where the time goes in v5:
time: 129 us
  blocking collectives  107 us (83%)
  Pallas kernels  15.3 us (12%)
  starting transfers between devices  3.83 us (3%)
  waiting for transfers between devices  1.9 us (1%)
    all_to_all x1, blocking collectives, per_device(): parts = lax.all_to_all(parts, 'z', 0, 0, tiled=True)  36.3 us
    all_to_all x1, blocking collectives, per_device(): shares = lax.all_to_all(part, vocab, 0, 0, tiled=True)  27.9 us
    all_gather x1, blocking collectives, per_device(): own = lax.all_gather(soften(index, parts, target), 'z', axis=1)  26.2 us
    all_to_all x1, blocking collectives, per_device(): reduced = lax.all_to_all(spread, vocab, 0, 0, tiled=True)  16.7 us
    pallas_call x2, Pallas kernels, half_grad(): call(inside, out, [smem] + [vmem] * (4 + len(before)), scratch)  4.74 us
    pallas_call x1, Pallas kernels, finish(): call(kernel, [jax.ShapeDtypeStruct((depth, tokens), bf16), jax.ShapeDtype...  3.52 us
    pallas_call x1, Pallas kernels, sent_logits(): pl.pallas_call(kernel, in_specs=[smem, hbm, hbm], out_specs=vmem, out_sha...  2.83 us
  transfers between devices with their start and end apart: 2, of which 2 were waited for; matrix products, arithmetic and copies ran while one was open for 0% of the time, Pallas kernels for 2%

profile of v5, /device:TPU:8, one launch (start us, length us, event | category | flops | bytes accessed | tf_op | source)
XLA Modules:
  0.0 129.0 jit_solution(16850516308760082883)
XLA Ops:
  0.6 0.0 copy-start
  0.6 0.0 copy-start.1
  0.7 0.0 copy-start.4
  0.7 0.0 copy-start.3
  0.7 0.0 copy-start.2
  0.7 2.8 %shard_map.77 = bf16[8,448,128]{2,1,0:T(8,128)(2,1)} custom-call(s32[1]{0:T(128)} %bitcast.index_ref, bf16[288,448]{1,0:T(8,128)(2,1)} %bitcast.20, bf16[288,2048]{1,0:T(8,128)(2,1)} %bitcast.13), custom_call_target="tpu_custom_call" | custom-call | tf_op jit(solution)/shard_map/pallas_call | solution.py:71
  3.5 1.9 %collective-permute-start = (bf16[8,448,128]{2,1,0:T(8,128)(2,1)}, bf16[8,448,128]{2,1,0:T(8,128)(2,1)S(1)}, u32[]{:S(2)}, u32[]{:S(2)}) collective-permute-start(bf16[8,448,128]{2,1,0:T(8,128)(2,1)} %shard_map.77), channel_id=1, source_target_pairs={{0,1},{1,0},{2,3},{3,2},{4,5},{5,4},{6,7},{7,6},{8,9},{9,8},{10,11... | collective-permute-start | bytes 2752520 | tf_op jit(solution)/shard_map/ppermute | solution.py:358
  5.5 0.1 pad_add_fusion.index_ref.refs_0_
  5.5 0.0 copy-done
  5.5 0.0 copy-done.1
  5.5 0.0 copy-done.4
  5.6 0.0 copy-done.3
  5.6 0.0 copy-done.2
  5.6 1.2 shard_map.76
  6.8 1.3 collective-permute-done.received_ref
  8.1 0.2 shard_map.78
  8.3 36.3 %all_to_all.15.parts_ref = bf16[8,448,128]{2,1,0:T(8,128)(2,1)S(1)} all-to-all(bf16[8,448,128]{2,1,0:T(8,128)(2,1)S(1)} %shard_map.78), channel_id=1, replica_groups=mesh['x'=4,'y'=8,'z'=8,'core'=2] {'z'}, dimensions={0} | all-to-all | bytes 1835008 | tf_op jit(solution)/shard_map/all_to_all | solution.py:361
  44.6 1.3 %shard_map.79 = bf16[29,16,128]{2,1,0:T(8,128)(2,1)S(1)} custom-call(s32[4]{0:T(128)S(1)} %pad_add_fusion.index_ref.refs_0_, bf16[8,448,128]{2,1,0:T(8,128)(2,1)S(1)} %all_to_all.15.parts_ref, f32[448,128]{1,0:T(8,128)S(1)} %get-tuple-element.14.target_ref.refs_2_), custom_call_target="tpu_custom_call" | custom-call | tf_op jit(solution)/shard_map/pallas_call | solution.py:193
  45.9 26.2 %all-gather = bf16[29,128,128]{2,1,0:T(8,128)(2,1)S(1)} all-gather(bf16[29,16,128]{2,1,0:T(8,128)(2,1)S(1)} %shard_map.79), channel_id=2, replica_groups=mesh['x'=4,'y'=8,'z'=8,'core'=2] {'z'}, dimensions={1}, use_global_device_ids=true | all-gather | bytes 1069056 | tf_op jit(solution)/shard_map/all_gather | solution.py:362
  72.1 1.9 %collective-permute-start.1 = (bf16[29,8,16,128]{3,2,1,0:T(8,128)(2,1)S(1)}, bf16[29,8,16,128]{3,2,1,0:T(8,128)(2,1)S(1)}, u32[]{:S(2)}, u32[]{:S(2)}) collective-permute-start(bf16[29,8,16,128]{3,2,1,0:T(8,128)(2,1)S(1)} %bitcast.17), channel_id=1, source_target_pairs={{0,1},{1,0},{2,3},{3,2},{4,5},{5,4},{6,7},{7,6},{8,9},{9,8},{10,11... | collective-permute-start | bytes 2850824 | tf_op jit(solution)/shard_map/ppermute | solution.py:363
  74.0 1.9 %shard_map.80 = (f32[896,288]{1,0:T(8,128)S(1)}, f32[16,128]{1,0:T(8,128)S(1)}) custom-call(s32[4]{0:T(128)S(1)} %pad_add_fusion.index_ref.refs_0_, bf16[29,8,16,128]{3,2,1,0:T(8,128)(2,1)S(1)} %bitcast.18, f32[448,128]{1,0:T(8,128)S(1)} %get-tuple-element.14.target_ref.refs_2_, f32[512,128]{1,0:T(8,128)S(1)} %get-tuple-element.15.refs_3_.small_ref, ...), custom_call_target="tpu_custom_call" | custom-call | tf_op jit(solution)/shard_map/pallas_call | solution.py:263
  75.9 0.6 collective-permute-done.1.soft_ref.other_ref
  76.5 2.9 %shard_map.81 = (bf16[32,16,512]{2,1,0:T(8,128)(2,1)S(1)}, f32[448,128]{1,0:T(8,128)S(1)}) custom-call(s32[4]{0:T(128)S(1)} %pad_add_fusion.index_ref.refs_0_, bf16[29,8,16,128]{3,2,1,0:T(8,128)(2,1)S(1)} %collective-permute-done.1.soft_ref.other_ref, f32[448,128]{1,0:T(8,128)S(1)} %get-tuple-element.14.target_ref.refs_2_, ...), custom_call_target="tpu_custom_call" | custom-call | tf_op jit(solution)/shard_map/pallas_call | solution.py:263
  79.4 27.9 %all_to_all.16.parts_ref = bf16[32,16,512]{2,1,0:T(8,128)(2,1)S(1)} all-to-all(bf16[32,16,512]{2,1,0:T(8,128)(2,1)S(1)} %get-tuple-element.18), channel_id=1, replica_groups=mesh['x'=4,'y'=8,'z'=8,'core'=2] {'x','y'}, dimensions={0} | all-to-all | bytes 1048576 | tf_op jit(solution)/shard_map/all_to_all | solution.py:366
  107.3 1.5 %shard_map.82 = bf16[32,16,256]{2,1,0:T(8,128)(2,1)S(1)} custom-call(s32[4]{0:T(128)S(1)} %pad_add_fusion.index_ref.refs_0_, bf16[32,16,512]{2,1,0:T(8,128)(2,1)S(1)} %all_to_all.16.parts_ref, f32[512,128]{1,0:T(8,128)S(1)} %get-tuple-element.15.refs_3_.small_ref), custom_call_target="tpu_custom_call" | custom-call | tf_op jit(solution)/shard_map/pallas_call | solution.py:300
  108.8 16.7 %all_to_all.17.reduced_ref = bf16[32,16,256]{2,1,0:T(8,128)(2,1)S(1)} all-to-all(bf16[32,16,256]{2,1,0:T(8,128)(2,1)S(1)} %shard_map.82), channel_id=1, replica_groups=mesh['x'=4,'y'=8,'z'=8,'core'=2] {'x','y'}, dimensions={0} | all-to-all | bytes 524288 | tf_op jit(solution)/shard_map/all_to_all | solution.py:368
  125.5 3.5 %shard_map.83 = (bf16[288,448]{1,0:T(8,128)(2,1)}, bf16[288,2048]{1,0:T(8,128)(2,1)}, f32[1,28]{1,0:T(1,128)}) custom-call(s32[4]{0:T(128)S(1)} %pad_add_fusion.index_ref.refs_0_, bf16[32,16,256]{2,1,0:T(8,128)(2,1)S(1)} %all_to_all.17.reduced_ref, bf16[29,8,16,128]{3,2,1,0:T(8,128)(2,1)S(1)} %bitcast.19, ...), custom_call_target="tpu_custom_call" | custom-call | tf_op jit(solution)/shard_map/pallas_call | solution.py:337
Async XLA Ops:
  0.6 4.9 %copy-start = (bf16[2048,288]{0,1:T(8,128)(2,1)S(1)}, bf16[2048,288]{0,1:T(8,128)(2,1)}, u32[]{:S(2)}) copy-start(bf16[2048,288]{0,1:T(8,128)(2,1)} %param.6) | copy-start | bytes 3538948
  0.6 4.9 %copy-start.1 = (bf16[448,288]{0,1:T(8,128)(2,1)S(1)}, bf16[448,288]{0,1:T(8,128)(2,1)}, u32[]{:S(2)}) copy-start(bf16[448,288]{0,1:T(8,128)(2,1)} %param.5) | copy-start | bytes 774148
  0.7 4.9 %copy-start.4 = (f32[448]{0:T(512)S(1)}, f32[448]{0:T(512)}, u32[]{:S(2)}) copy-start(f32[448]{0:T(512)} %param.9) | copy-start | bytes 5380
  0.7 4.9 %copy-start.3 = (f32[448]{0:T(512)S(1)}, f32[448]{0:T(512)}, u32[]{:S(2)}) copy-start(f32[448]{0:T(512)} %param.8) | copy-start | bytes 5380
  0.7 4.9 %copy-start.2 = (s32[448]{0:T(512)S(1)}, s32[448]{0:T(512)}, u32[]{:S(2)}) copy-start(s32[448]{0:T(512)} %param.7) | copy-start | bytes 5380
  3.5 4.6 %collective-permute-start = (bf16[8,448,128]{2,1,0:T(8,128)(2,1)}, bf16[8,448,128]{2,1,0:T(8,128)(2,1)S(1)}, u32[]{:S(2)}, u32[]{:S(2)}) collective-permute-start(bf16[8,448,128]{2,1,0:T(8,128)(2,1)} %shard_map.77), channel_id=1, source_target_pairs={{0,1},{1,0},{2,3},{3,2},{4,5},{5,4},{6,7},{7,6},{8,9},{9,8},{10,11... | collective-permute-start | bytes 2752520 | tf_op jit(solution)/shard_map/ppermute | solution.py:358
  72.1 4.4 %collective-permute-start.1 = (bf16[29,8,16,128]{3,2,1,0:T(8,128)(2,1)S(1)}, bf16[29,8,16,128]{3,2,1,0:T(8,128)(2,1)S(1)}, u32[]{:S(2)}, u32[]{:S(2)}) collective-permute-start(bf16[29,8,16,128]{3,2,1,0:T(8,128)(2,1)S(1)} %bitcast.17), channel_id=1, source_target_pairs={{0,1},{1,0},{2,3},{3,2},{4,5},{5,4},{6,7},{7,6},{8,9},{9,8},{10,11... | collective-permute-start | bytes 2850824 | tf_op jit(solution)/shard_map/ppermute | solution.py:363

commit v6 on v5

--- a/solution.py
+++ b/solution.py
@@ -83,7 +83,10 @@
 
 
 def kept_logits(index, hidden_t, weight_t, vectors):
-    def kernel(index_ref, h_ref, w_ref, target_ref, rest_ref, cot_ref, out_ref, wanted_ref, small_ref):
+    def kernel(
+        index_ref, h_ref, w_ref, target_ref, rest_ref, cot_ref,
+        out_ref, wanted_ref, small_ref, pack_ref, unpack_ref,
+    ):
         rows = rows_of(target_ref[...].astype(f32)) + rows_of(rest_ref[...]) + rows_of(cot_ref[...])
         tile = jnp.zeros((16, lanes), f32)
         for r, row in enumerate(rows):
@@ -98,11 +101,18 @@
             part = jnp.dot(h, w_ref[:, pl.ds(at, 256)], preferred_element_type=f32)
             out_ref[2 * i] = part[:, :lanes]
             out_ref[2 * i + 1] = part[:, lanes:]
+        for axis, ref in enumerate((pack_ref, unpack_ref)):
+            token, group = places(axis)
+            each = iota((tokens, 1) if axis else (1, tokens), 1 - axis)
+            choose = [ones_where(token == each.astype(f32)), ones_where(group == divided(each, tail_rows)[0])]
+            ref[...] = jnp.concatenate(choose, axis=1 - axis)
 
     out = [
         jax.ShapeDtypeStruct((8, tokens, lanes), f32),
         jax.ShapeDtypeStruct((tokens, lanes), f32),
         jax.ShapeDtypeStruct((shards * chunk, lanes), f32),
+        jax.ShapeDtypeStruct((shards * chunk, 2 * tokens), bf16),
+        jax.ShapeDtypeStruct((2 * tokens, shards * chunk), bf16),
     ]
     return call(kernel, out, [smem] + [vmem] * 5)(index, hidden_t, weight_t, *vectors)
 
@@ -115,12 +125,17 @@
     return call(kernel, jax.ShapeDtypeStruct(kept.shape, bf16), [vmem, vmem])(kept, received)
 
 
+def divided(count, by):
+    count = count.astype(f32)
+    quotient = jnp.floor((count + 0.5) * (1.0 / by))
+    return quotient, count - quotient * by
+
+
 def places(axis):
     shape = (shards * chunk, 1) if axis == 0 else (1, shards * chunk)
-    row = iota(shape, axis)
-    number, inside = row // chunk, row % chunk
-    token = jnp.where(inside < share, number * share + inside, -1)
-    group = jnp.where(inside < share, -1, number * 2 + inside - share)
+    number, inside = divided(iota(shape, axis), chunk)
+    token = jnp.where(inside < share, number * share + inside, -1.0)
+    group = jnp.where(inside < share, -1.0, number * 2 + inside - share)
     return token, group
 
 
@@ -129,26 +144,22 @@
 
 
 def exact(a, b):
-    wide = a.dtype == f32 or b.dtype == f32
-    precision = lax.Precision.HIGHEST if wide else None
-    return jnp.dot(a, b, precision=precision, preferred_element_type=f32)
+    return jnp.dot(a, b, preferred_element_type=f32)
 
 
 def repeated(tail, width, lanes_out, member):
-    lane = iota((lanes, lanes_out), 1)
-    spread = (lane % width == iota((lanes, lanes_out), 0)) & (lane < width * tail_rows)
-    slot = iota((1, lanes_out), 1) // width
+    slot, place = divided(iota((1, lanes_out), 1), width)
+    spread = jnp.where(slot < tail_rows, place, -1.0) == iota((lanes, lanes_out), 0).astype(f32)
     return jnp.where(slot == member, exact(tail, ones_where(spread)), 0.0).astype(bf16)
 
 
 def folded(wide, width, member):
     lanes_in = wide.shape[1]
-    lane = iota((lanes_in, lanes), 0)
-    fold = (lane % width == iota((lanes_in, lanes), 1)) & (lane < width * tail_rows)
-    slot = iota((1, lanes_in), 1) // width
+    slot, place = divided(iota((lanes_in, 1), 0), width)
+    fold = jnp.where(slot < tail_rows, place, -1.0) == iota((1, lanes), 1).astype(f32)
+    slot = divided(iota((1, lanes_in), 1), width)[0]
     mine = jnp.where(slot == member, wide, 0.0)
-    fold = jnp.where(fold, 1.0, 0.0)
-    return exact(mine, fold) if mine.dtype == f32 else exact(mine, fold.astype(bf16))
+    return exact(mine, ones_where(fold))
 
 
 def high_low(tile):
@@ -171,10 +182,9 @@
 
         def total(block):
             return lax.dot_general(
-                jnp.ones((8, lanes), f32),
-                block,
+                jnp.ones((16, 2 * lanes), bf16),
+                jnp.concatenate([part.astype(bf16) for part in high_low(block)], axis=1),
                 (((1,), (1,)), ((), ())),
-                precision=lax.Precision.HIGHEST,
                 preferred_element_type=f32,
             )[0:1]
 
@@ -233,19 +243,16 @@
         if not last:
             refs[1][...] = sums
             return
-        out_ref, hits_ref = refs[2:4]
+        pack_ref, out_ref, hits_ref = refs[2:5]
         hits_ref[...] = hits
         first, second = total[:tokens], total[tokens:]
         lane = iota((tokens, lanes), 1)
         tail = jnp.concatenate([second[:, 224:], jnp.zeros((tokens, lanes - depth + 224), f32)], axis=1)
         for k, column in enumerate(high_low(power) + high_low(picked)):
             tail = jnp.where(lane == depth - 224 + k, column, tail)
-        tail = repeated(tail.astype(bf16), depth - 220, 512, iota((tokens, 1), 0) % tail_rows)
+        tail = repeated(tail.astype(bf16), depth - 220, 512, divided(iota((tokens, 1), 0), tail_rows)[1])
         main = jnp.concatenate([first, second[:, :224]], axis=1).astype(bf16)
-        token, group = places(0)
-        each = iota((1, tokens), 1)
-        choose = [ones_where(token == each), ones_where(group == each // tail_rows)]
-        out = exact(jnp.concatenate(choose, axis=1), jnp.concatenate([main, tail], axis=0))
+        out = exact(pack_ref[...], jnp.concatenate([main, tail], axis=0))
         out_ref[...] = out.astype(bf16).reshape(shards, chunk, 512)
 
     total = (2 * tokens, depth)
@@ -272,10 +279,13 @@
             total = total + parts_ref[i].astype(f32)
         mine = small_ref[pl.ds(index_ref[3] * share, chunk)]
         rest, cot = mine[:, 0:1], mine[:, 1:2]
-        row, column = iota((chunk, 1), 0), iota((1, chunk), 1)
-        own = (column == share + row // tail_rows) & (row < share)
-        held = exact(jnp.where(own, 1.0, 0.0), total)
-        tail = folded(held, depth - 220, row % tail_rows)
+        row = iota((chunk, 1), 0)
+        group, member = divided(row, tail_rows)
+        held = jnp.where(row < tail_rows, total[share : share + 1], total[share + 1 : share + 2])
+        width = depth - 220
+        tail = jnp.zeros((chunk, width), f32)
+        for k in range(tail_rows):
+            tail = jnp.where(member == k, held[:, k * width : (k + 1) * width], tail)
         at = depth - 224
         power = tail[:, at : at + 1] + tail[:, at + 1 : at + 2]
         picked = tail[:, at + 2 : at + 3] + tail[:, at + 3 : at + 4]
@@ -290,9 +300,12 @@
         lane = iota((chunk, lanes), 1)
         for k, column_k in enumerate(high_low(scale) + high_low(loss)):
             end = jnp.where((lane == depth - 256 + k) & (row < share), column_k, end)
-        end = repeated(end.astype(bf16), depth - 252, 256, row % tail_rows)
-        into = ones_where((row == share + column // tail_rows) & (column < share))
-        out = (out[:, :256] + exact(into, end)).astype(bf16)
+        end = repeated(end.astype(bf16), depth - 252, 256, member).astype(f32)
+        out = out[:, :256]
+        for k in range(2):
+            ends = jnp.sum(jnp.where(group == k, end, 0.0), axis=0, keepdims=True)
+            out = jnp.where(row == share + k, ends, out)
+        out = out.astype(bf16)
         for i in range(shards):
             out_ref[i] = out
 
@@ -300,19 +313,16 @@
     return call(kernel, out, [smem, vmem, vmem])(index, parts, small)
 
 
-def finish(index, reduced, own, other, hits, target, hidden_t):
+def finish(index, reduced, own, other, hits, target, unpack, hidden_t):
     depth = hidden_t.shape[0]
     losses_each = tokens // 16
 
     def kernel(
-        index_ref, reduced_ref, own_ref, other_ref, hits_ref, target_ref, h_ref,
+        index_ref, reduced_ref, own_ref, other_ref, hits_ref, target_ref, unpack_ref, h_ref,
         gh_ref, gw_ref, loss_ref, scales, losses,
     ):
-        token, group = places(1)
-        each = iota((tokens, 1), 0)
-        choose = [ones_where(token == each), ones_where(group == each // tail_rows)]
-        held = exact(jnp.concatenate(choose, axis=0), reduced_ref[...].reshape(shards * chunk, 256))
-        last = folded(held[tokens:].astype(bf16), depth - 252, each % tail_rows)
+        held = exact(unpack_ref[...], reduced_ref[...].reshape(shards * chunk, 256))
+        last = folded(held[tokens:].astype(bf16), depth - 252, divided(iota((tokens, 1), 0), tail_rows)[1])
         at = depth - 256
         scales[...] = jnp.broadcast_to(last[:, at : at + 1] + last[:, at + 1 : at + 2], (tokens, lanes))
         losses[:tokens] = jnp.broadcast_to(last[:, at + 2 : at + 3] + last[:, at + 3 : at + 4], (tokens, lanes))
@@ -341,9 +351,9 @@
             jax.ShapeDtypeStruct((depth, 2048), bf16),
             jax.ShapeDtypeStruct((1, losses_each), f32),
         ],
-        [smem] + [vmem] * 6,
+        [smem] + [vmem] * 7,
         [pltpu.VMEM((tokens, lanes), f32), pltpu.VMEM((tokens + 32, lanes), f32)],
-    )(index, reduced, own, other, hits, target, hidden_t)
+    )(index, reduced, own, other, hits, target, unpack, hidden_t)
 
 
 def per_device(hidden, head_weight, targets, lse_rest, cotangent):
@@ -356,18 +366,18 @@
     vectors = [v.reshape(1, tokens) for v in (targets, lse_rest, cotangent)]
 
     received = lax.ppermute(sent_logits(core.reshape(1), hidden_t, weight_t), "core", swap)
-    kept, target, small = kept_logits(index, hidden_t, weight_t, vectors)
+    kept, target, small, pack, unpack = kept_logits(index, hidden_t, weight_t, vectors)
     parts = add_halves(kept, received)
     parts = lax.all_to_all(parts, "z", 0, 0, tiled=True)
     own = lax.all_gather(soften(index, parts, target), "z", axis=1)
     other = lax.ppermute(own, "core", swap)
     before = half_grad(index, own, target, small, weight_t)
-    part, hits = half_grad(index, other, target, small, weight_t, before)
+    part, hits = half_grad(index, other, target, small, weight_t, (*before, pack))
     shares = lax.all_to_all(part, vocab, 0, 0, tiled=True)
     spread = reduce_chunk(index, shares, small, hidden.shape[1])
     reduced = lax.all_to_all(spread, vocab, 0, 0, tiled=True)
     grad_hidden, grad_weight, token_loss = finish(
-        index, reduced, own, other, hits, target, hidden_t
+        index, reduced, own, other, hits, target, unpack, hidden_t
     )
     return (grad_hidden.T, grad_weight.T, token_loss.reshape(-1))
 

time: 129 us -> 129 us (level)
  transfers between devices with their start and end apart: 2 -> 2, of which waited for: 2 -> 2; matrix products, arithmetic and copies ran while one was open for 0% -> 0% of each run, Pallas kernels for 2% -> 3%
where the time goes in v6:
time: 129 us; the launch traced here: 128 us
  blocking collectives  107 us (83%)
  Pallas kernels  15 us (12%)
  starting transfers between devices  3.83 us (3%)
  waiting for transfers between devices  1.58 us (1%)
    all_to_all x1, blocking collectives, per_device(): parts = lax.all_to_all(parts, 'z', 0, 0, tiled=True)  36.3 us
    all_to_all x1, blocking collectives, per_device(): shares = lax.all_to_all(part, vocab, 0, 0, tiled=True)  27.9 us
    all_gather x1, blocking collectives, per_device(): own = lax.all_gather(soften(index, parts, target), 'z', axis=1)  26.2 us
    all_to_all x1, blocking collectives, per_device(): reduced = lax.all_to_all(spread, vocab, 0, 0, tiled=True)  16.7 us
    pallas_call x2, Pallas kernels, half_grad(): call(inside, out, [smem] + [vmem] * (4 + len(before)), scratch)  4.53 us
    pallas_call x1, Pallas kernels, finish(): call(kernel, [jax.ShapeDtypeStruct((depth, tokens), bf16), jax.ShapeDtype...  3.53 us
    pallas_call x1, Pallas kernels, sent_logits(): pl.pallas_call(kernel, in_specs=[smem, hbm, hbm], out_specs=vmem, out_sha...  2.83 us
  transfers between devices with their start and end apart: 2, of which 2 were waited for; matrix products, arithmetic and copies ran while one was open for 0% of the time, Pallas kernels for 3%

profile of v6, /device:TPU:8, one launch (start us, length us, event | category | flops | bytes accessed | tf_op | source)
XLA Modules:
  0.0 128.4 jit_solution(5016982905861159341)
XLA Ops:
  0.6 0.0 copy-start
  0.6 0.0 copy-start.1
  0.7 0.0 copy-start.4
  0.7 0.0 copy-start.3
  0.7 0.0 copy-start.2
  0.7 2.8 %shard_map.77 = bf16[8,448,128]{2,1,0:T(8,128)(2,1)} custom-call(s32[1]{0:T(128)} %bitcast.index_ref, bf16[288,448]{1,0:T(8,128)(2,1)} %bitcast.20, bf16[288,2048]{1,0:T(8,128)(2,1)} %bitcast.13), custom_call_target="tpu_custom_call" | custom-call | tf_op jit(solution)/shard_map/pallas_call | solution.py:71
  3.5 1.9 %collective-permute-start = (bf16[8,448,128]{2,1,0:T(8,128)(2,1)}, bf16[8,448,128]{2,1,0:T(8,128)(2,1)S(1)}, u32[]{:S(2)}, u32[]{:S(2)}) collective-permute-start(bf16[8,448,128]{2,1,0:T(8,128)(2,1)} %shard_map.77), channel_id=1, source_target_pairs={{0,1},{1,0},{2,3},{3,2},{4,5},{5,4},{6,7},{7,6},{8,9},{9,8},{10,11... | collective-permute-start | bytes 2752520 | tf_op jit(solution)/shard_map/ppermute | solution.py:368
  5.5 0.1 pad_add_fusion.index_ref.refs_0_
  5.5 0.0 copy-done
  5.5 0.0 copy-done.1
  5.5 0.0 copy-done.4
  5.6 0.0 copy-done.3
  5.6 0.0 copy-done.2
  5.6 1.6 %shard_map.76 = (f32[8,448,128]{2,1,0:T(8,128)S(1)}, f32[448,128]{1,0:T(8,128)S(1)}, f32[512,128]{1,0:T(8,128)S(1)}, bf16[512,896]{1,0:T(8,128)(2,1)S(1)}, bf16[896,512]{1,0:T(8,128)(2,1)S(1)}) custom-call(s32[4]{0:T(128)S(1)} %pad_add_fusion.index_ref.refs_0_, bf16[288,448]{1,0:T(8,128)(2,1)S(1)} %bitcast.21, bf16[288,2048]{1,0:T(8,128)(2,1)S(1)} %bitcast.14, ...), custom_call_target="tpu_custom_call" | custom-call | tf_op jit(solution)/shard_map/pallas_call | solution.py:117
  7.2 0.9 collective-permute-done.received_ref
  8.1 0.2 shard_map.78
  8.3 36.3 %all_to_all.15.parts_ref = bf16[8,448,128]{2,1,0:T(8,128)(2,1)S(1)} all-to-all(bf16[8,448,128]{2,1,0:T(8,128)(2,1)S(1)} %shard_map.78), channel_id=1, replica_groups=mesh['x'=4,'y'=8,'z'=8,'core'=2] {'z'}, dimensions={0} | all-to-all | bytes 1835008 | tf_op jit(solution)/shard_map/all_to_all | solution.py:371
  44.6 0.9 shard_map.79
  45.6 26.2 %all-gather = bf16[29,128,128]{2,1,0:T(8,128)(2,1)S(1)} all-gather(bf16[29,16,128]{2,1,0:T(8,128)(2,1)S(1)} %shard_map.79), channel_id=2, replica_groups=mesh['x'=4,'y'=8,'z'=8,'core'=2] {'z'}, dimensions={1}, use_global_device_ids=true | all-gather | bytes 1069056 | tf_op jit(solution)/shard_map/all_gather | solution.py:372
  71.7 1.9 %collective-permute-start.1 = (bf16[29,8,16,128]{3,2,1,0:T(8,128)(2,1)S(1)}, bf16[29,8,16,128]{3,2,1,0:T(8,128)(2,1)S(1)}, u32[]{:S(2)}, u32[]{:S(2)}) collective-permute-start(bf16[29,8,16,128]{3,2,1,0:T(8,128)(2,1)S(1)} %bitcast.17), channel_id=1, source_target_pairs={{0,1},{1,0},{2,3},{3,2},{4,5},{5,4},{6,7},{7,6},{8,9},{9,8},{10,11... | collective-permute-start | bytes 2850824 | tf_op jit(solution)/shard_map/ppermute | solution.py:373
  73.7 1.8 %shard_map.80 = (f32[896,288]{1,0:T(8,128)S(1)}, f32[16,128]{1,0:T(8,128)S(1)}) custom-call(s32[4]{0:T(128)S(1)} %pad_add_fusion.index_ref.refs_0_, bf16[29,8,16,128]{3,2,1,0:T(8,128)(2,1)S(1)} %bitcast.18, f32[448,128]{1,0:T(8,128)S(1)} %get-tuple-element.16.target_ref.refs_2_, f32[512,128]{1,0:T(8,128)S(1)} %get-tuple-element.17.refs_3_.small_ref, ...), custom_call_target="tpu_custom_call" | custom-call | tf_op jit(solution)/shard_map/pallas_call | solution.py:270
  75.5 0.6 collective-permute-done.1.soft_ref.other_ref
  76.1 2.7 %shard_map.81 = (bf16[32,16,512]{2,1,0:T(8,128)(2,1)S(1)}, f32[448,128]{1,0:T(8,128)S(1)}) custom-call(s32[4]{0:T(128)S(1)} %pad_add_fusion.index_ref.refs_0_, bf16[29,8,16,128]{3,2,1,0:T(8,128)(2,1)S(1)} %collective-permute-done.1.soft_ref.other_ref, f32[448,128]{1,0:T(8,128)S(1)} %get-tuple-element.16.target_ref.refs_2_, ...), custom_call_target="tpu_custom_call" | custom-call | tf_op jit(solution)/shard_map/pallas_call | solution.py:270
  78.8 27.9 %all_to_all.16.parts_ref = bf16[32,16,512]{2,1,0:T(8,128)(2,1)S(1)} all-to-all(bf16[32,16,512]{2,1,0:T(8,128)(2,1)S(1)} %get-tuple-element.21), channel_id=1, replica_groups=mesh['x'=4,'y'=8,'z'=8,'core'=2] {'x','y'}, dimensions={0} | all-to-all | bytes 1048576 | tf_op jit(solution)/shard_map/all_to_all | solution.py:376
  106.7 1.4 %shard_map.82 = bf16[32,16,256]{2,1,0:T(8,128)(2,1)S(1)} custom-call(s32[4]{0:T(128)S(1)} %pad_add_fusion.index_ref.refs_0_, bf16[32,16,512]{2,1,0:T(8,128)(2,1)S(1)} %all_to_all.16.parts_ref, f32[512,128]{1,0:T(8,128)S(1)} %get-tuple-element.17.refs_3_.small_ref), custom_call_target="tpu_custom_call" | custom-call | tf_op jit(solution)/shard_map/pallas_call | solution.py:313
  108.1 16.7 %all_to_all.17.reduced_ref = bf16[32,16,256]{2,1,0:T(8,128)(2,1)S(1)} all-to-all(bf16[32,16,256]{2,1,0:T(8,128)(2,1)S(1)} %shard_map.82), channel_id=1, replica_groups=mesh['x'=4,'y'=8,'z'=8,'core'=2] {'x','y'}, dimensions={0} | all-to-all | bytes 524288 | tf_op jit(solution)/shard_map/all_to_all | solution.py:378
  124.8 3.5 %shard_map.83 = (bf16[288,448]{1,0:T(8,128)(2,1)}, bf16[288,2048]{1,0:T(8,128)(2,1)}, f32[1,28]{1,0:T(1,128)}) custom-call(s32[4]{0:T(128)S(1)} %pad_add_fusion.index_ref.refs_0_, bf16[32,16,256]{2,1,0:T(8,128)(2,1)S(1)} %all_to_all.17.reduced_ref, bf16[29,8,16,128]{3,2,1,0:T(8,128)(2,1)S(1)} %bitcast.19, ...), custom_call_target="tpu_custom_call" | custom-call | tf_op jit(solution)/shard_map/pallas_call | solution.py:347
Async XLA Ops:
  0.6 4.9 %copy-start = (bf16[2048,288]{0,1:T(8,128)(2,1)S(1)}, bf16[2048,288]{0,1:T(8,128)(2,1)}, u32[]{:S(2)}) copy-start(bf16[2048,288]{0,1:T(8,128)(2,1)} %param.6) | copy-start | bytes 3538948
  0.6 4.9 %copy-start.1 = (bf16[448,288]{0,1:T(8,128)(2,1)S(1)}, bf16[448,288]{0,1:T(8,128)(2,1)}, u32[]{:S(2)}) copy-start(bf16[448,288]{0,1:T(8,128)(2,1)} %param.5) | copy-start | bytes 774148
  0.7 4.9 %copy-start.4 = (f32[448]{0:T(512)S(1)}, f32[448]{0:T(512)}, u32[]{:S(2)}) copy-start(f32[448]{0:T(512)} %param.9) | copy-start | bytes 5380
  0.7 4.9 %copy-start.3 = (f32[448]{0:T(512)S(1)}, f32[448]{0:T(512)}, u32[]{:S(2)}) copy-start(f32[448]{0:T(512)} %param.8) | copy-start | bytes 5380
  0.7 4.9 %copy-start.2 = (s32[448]{0:T(512)S(1)}, s32[448]{0:T(512)}, u32[]{:S(2)}) copy-start(s32[448]{0:T(512)} %param.7) | copy-start | bytes 5380
  3.5 4.6 %collective-permute-start = (bf16[8,448,128]{2,1,0:T(8,128)(2,1)}, bf16[8,448,128]{2,1,0:T(8,128)(2,1)S(1)}, u32[]{:S(2)}, u32[]{:S(2)}) collective-permute-start(bf16[8,448,128]{2,1,0:T(8,128)(2,1)} %shard_map.77), channel_id=1, source_target_pairs={{0,1},{1,0},{2,3},{3,2},{4,5},{5,4},{6,7},{7,6},{8,9},{9,8},{10,11... | collective-permute-start | bytes 2752520 | tf_op jit(solution)/shard_map/ppermute | solution.py:368
  71.7 4.4 %collective-permute-start.1 = (bf16[29,8,16,128]{3,2,1,0:T(8,128)(2,1)S(1)}, bf16[29,8,16,128]{3,2,1,0:T(8,128)(2,1)S(1)}, u32[]{:S(2)}, u32[]{:S(2)}) collective-permute-start(bf16[29,8,16,128]{3,2,1,0:T(8,128)(2,1)S(1)} %bitcast.17), channel_id=1, source_target_pairs={{0,1},{1,0},{2,3},{3,2},{4,5},{5,4},{6,7},{7,6},{8,9},{9,8},{10,11... | collective-permute-start | bytes 2850824 | tf_op jit(solution)/shard_map/ppermute | solution.py:373
